TPU v7x, 32 devices: a whole 2x2x4 slice. The times are simulated.
32 devices in a mesh: fsdp: 8 (over z, y), ctx: 4 (over x, core).
Axes of the slice: x: 2, y: 2, z: 4, core: 2. Of those that a mesh axis runs over, the one named last changes fastest.
Arguments:
- tokens: bfloat16 [8, 512, 640], P('fsdp', 'ctx'), may hold values from -6 to 6
- positions: int32 [8, 512], P('fsdp', 'ctx'), may hold values from 0 to 511, as said below
- cotangent: bfloat16 [8, 512, 640], P('fsdp', 'ctx'), may hold values from -6 to 6
- attn_norm: bfloat16 [640], P('fsdp'), may hold values from 0.099609375 to 1.8984375
- w_query: bfloat16 [640, 1024], P('fsdp'), may hold values from -0.25 to 0.25
- w_key: bfloat16 [640, 256], P('fsdp'), may hold values from -0.25 to 0.25
- w_value: bfloat16 [640, 256], P('fsdp'), may hold values from -0.25 to 0.25
- query_norm: bfloat16 [256], P('fsdp'), may hold values from 0.099609375 to 1.8984375
- key_norm: bfloat16 [256], P('fsdp'), may hold values from 0.099609375 to 1.8984375
- w_output: bfloat16 [1024, 640], P('fsdp'), may hold values from -0.1875 to 0.1875
- attn_post_norm: bfloat16 [640], P('fsdp'), may hold values from 0.099609375 to 1.8984375
- ffn_norm: bfloat16 [640], P('fsdp'), may hold values from 0.099609375 to 1.8984375
- w_gate: bfloat16 [640, 2048], P('fsdp'), may hold values from -0.25 to 0.25
- w_up: bfloat16 [640, 2048], P('fsdp'), may hold values from -0.25 to 0.25
- w_down: bfloat16 [2048, 640], P('fsdp'), may hold values from -0.125 to 0.125
- ffn_post_norm: bfloat16 [640], P('fsdp'), may hold values from 0.099609375 to 1.8984375
Outputs:
- layer_out: bfloat16 [8, 512, 640], P('fsdp', 'ctx')
- tokens_grad: bfloat16 [8, 512, 640], P('fsdp', 'ctx')
- attn_norm_grad: float32 [640], P('fsdp')
- w_query_grad: float32 [640, 1024], P('fsdp')
- w_key_grad: float32 [640, 256], P('fsdp')
- w_value_grad: float32 [640, 256], P('fsdp')
- query_norm_grad: float32 [256], P('fsdp')
- key_norm_grad: float32 [256], P('fsdp')
- w_output_grad: float32 [1024, 640], P('fsdp')
- attn_post_norm_grad: float32 [640], P('fsdp')
- ffn_norm_grad: float32 [640], P('fsdp')
- w_gate_grad: float32 [640, 2048], P('fsdp')
- w_up_grad: float32 [640, 2048], P('fsdp')
- w_down_grad: float32 [2048, 640], P('fsdp')
- ffn_post_norm_grad: float32 [640], P('fsdp')
Inputs may be any that keep to these rules, and one draw needn't show every extreme that they name: positions restart at 0 where a document begins and rise by one per token inside it; documents are consecutive runs of a sequence, so a token's position never exceeds its index in the sequence. Documents are mostly 200 to 2000 tokens, but a sequence's last document may be cut short, and one sequence starts and ends with documents of 1 to 63 tokens; some sequence is one whole document.
All inputs are finite; a program needn't handle non-finite values.
Results may differ from a plain program's by a relative error of at most 0.015.
Values may be sent and summed in bfloat16 or wider, within the bound.
A program may use at most 128 MiB of HBM per device.

v0:
```python
import jax
import jax.numpy as jnp
from jax import lax
from jax.sharding import PartitionSpec as P

HQ = 4
HD = 256
WINDOW = 512


EPSILON = 1e-06
ATTN_SCALE = 0.0625
NEGATIVE = -1e30


def shifted_2(value, axis, steps):
    count = lax.axis_size(axis)
    leading, last = (max(0, -steps), min(count, count - steps))
    return lax.ppermute(value, axis, [(source, source + steps) for source in range(leading, last)])


def rms_gain(values, gain_vec):
    return (
        values * lax.rsqrt(jnp.mean(values * values, axis=-1, keepdims=True) + EPSILON) * gain_vec
    )


def rope_tables(seq_place):
    half_width = HD // 2
    inverse = jnp.power(10000.0, -jnp.arange(half_width, dtype=jnp.float32) * (2.0 / HD))
    angles = seq_place.astype(jnp.float32)[:, None] * inverse[None, :]
    return (jnp.cos(angles)[:, None, :], jnp.sin(angles)[:, None, :])


def rotate(values, cosine, sine_table):
    half_width = values.shape[-1] // 2
    front_half = values[..., :half_width]
    back_half = values[..., half_width:]
    return jnp.concatenate(
        [
            front_half * cosine - back_half * sine_table,
            back_half * cosine + front_half * sine_table,
        ],
        axis=-1,
    )


def query_key(q_pre, k_pre, g_query, g_key, cosine, sine_table):
    return (
        rotate(rms_gain(q_pre, g_query), cosine, sine_table),
        rotate(rms_gain(k_pre, g_key), cosine, sine_table),
    )


def gated_gelu(gate_proj, up_proj):
    return jax.nn.gelu(gate_proj, approximate=True) * up_proj


def masked_scores(q_low, key_rows, key_mask):
    raw_scores = (
        jnp.einsum("thd,kd->htk", q_low, key_rows, preferred_element_type=jnp.float32) * ATTN_SCALE
    )
    return jnp.where(key_mask[None], raw_scores, NEGATIVE)


def body(
    tokens,
    positions,
    cotangent,
    attn_norm,
    w_query,
    w_key,
    w_value,
    query_norm,
    key_norm,
    w_output,
    attn_post_norm,
    ffn_norm,
    w_gate,
    w_up,
    w_down,
    ffn_post_norm,
):
    f32 = jnp.float32
    bf16 = jnp.bfloat16
    tok_rows = tokens.shape[1]
    model_width = tokens.shape[2]
    inputs = tokens.reshape(tok_rows, model_width).astype(f32)
    grad_out = cotangent.reshape(tok_rows, model_width).astype(f32)
    seq_place = positions.reshape(tok_rows)
    g_attn, wq_full, wk_full, wv_full, gq_full, gk_full, wo_full, g_attn_post = (
        lax.all_gather(attn_norm, "fsdp", axis=0, tiled=True),
        lax.all_gather(w_query, "fsdp", axis=0, tiled=True),
        lax.all_gather(w_key, "fsdp", axis=0, tiled=True),
        lax.all_gather(w_value, "fsdp", axis=0, tiled=True),
        lax.all_gather(query_norm, "fsdp", axis=0, tiled=True),
        lax.all_gather(key_norm, "fsdp", axis=0, tiled=True),
        lax.all_gather(w_output, "fsdp", axis=0, tiled=True),
        lax.all_gather(attn_post_norm, "fsdp", axis=0, tiled=True),
    )
    block_index = lax.axis_index("ctx")
    halo_count = -(-WINDOW // tok_rows)
    query_index = block_index * tok_rows + jnp.arange(tok_rows, dtype=jnp.int32)
    key_index = block_index * tok_rows + jnp.arange(
        -halo_count * tok_rows, tok_rows, dtype=jnp.int32
    )
    key_mask = (
        (key_index[None, :] <= query_index[:, None])
        & (query_index[:, None] - key_index[None, :] < WINDOW)
        & (key_index[None, :] >= (query_index - seq_place)[:, None])
    )
    attn_in = rms_gain(inputs, g_attn.astype(f32)).astype(bf16)
    q_pre = jnp.dot(attn_in, wq_full, preferred_element_type=f32).reshape(tok_rows, HQ, HD)
    k_pre = jnp.dot(attn_in, wk_full, preferred_element_type=f32).reshape(tok_rows, 1, HD)
    v_low = jnp.dot(attn_in, wv_full, preferred_element_type=f32).astype(bf16)
    cosine, sine_table = rope_tables(seq_place)
    gq_gain = gq_full.astype(f32)
    gk_gain = gk_full.astype(f32)
    q_turned, k_turned = query_key(q_pre, k_pre, gq_gain, gk_gain, cosine, sine_table)
    q_low = q_turned.astype(bf16)
    k_low = k_turned.reshape(tok_rows, HD).astype(bf16)
    key_parts = []
    value_parts = []
    for distance in range(halo_count, 0, -1):
        got_keys, got_values = shifted_2((k_low, v_low), "ctx", distance)
        key_parts.append(got_keys)
        value_parts.append(got_values)
    key_rows = jnp.concatenate(key_parts + [k_low], axis=0)
    value_rows = jnp.concatenate(value_parts + [v_low], axis=0)
    scores = masked_scores(q_low, key_rows, key_mask)
    row_max = jnp.max(scores, axis=-1, keepdims=True)
    shifted = jnp.exp(scores - row_max)
    row_total = jnp.sum(shifted, axis=-1, keepdims=True)
    log_total = row_max + jnp.log(row_total)
    prob_low = (shifted / row_total).astype(bf16)
    attended = jnp.einsum("htk,kd->thd", prob_low, value_rows, preferred_element_type=f32)
    att_low = attended.reshape(tok_rows, HQ * HD).astype(bf16)
    attn_branch = jnp.dot(att_low, wo_full, preferred_element_type=f32)
    g_post_gain = g_attn_post.astype(f32)
    hidden_res = inputs + rms_gain(attn_branch, g_post_gain)
    g_ffn, wg_full, wu_full, wd_full, g_ffn_post = (
        lax.all_gather(ffn_norm, "fsdp", axis=0, tiled=True),
        lax.all_gather(w_gate, "fsdp", axis=0, tiled=True),
        lax.all_gather(w_up, "fsdp", axis=0, tiled=True),
        lax.all_gather(w_down, "fsdp", axis=0, tiled=True),
        lax.all_gather(ffn_post_norm, "fsdp", axis=0, tiled=True),
    )
    g_ffn_gain = g_ffn.astype(f32)
    g_ffn_post_gain = g_ffn_post.astype(f32)
    ffn_in = rms_gain(hidden_res, g_ffn_gain).astype(bf16)
    gate_proj = jnp.dot(ffn_in, wg_full, preferred_element_type=f32)
    up_proj = jnp.dot(ffn_in, wu_full, preferred_element_type=f32)
    mixed_low = gated_gelu(gate_proj, up_proj).astype(bf16)
    down_out = jnp.dot(mixed_low, wd_full, preferred_element_type=f32)
    layer_out = hidden_res + rms_gain(down_out, g_ffn_post_gain)
    g_ffn, wg_full, wu_full, wd_full, g_ffn_post = (
        lax.all_gather(ffn_norm, "fsdp", axis=0, tiled=True),
        lax.all_gather(w_gate, "fsdp", axis=0, tiled=True),
        lax.all_gather(w_up, "fsdp", axis=0, tiled=True),
        lax.all_gather(w_down, "fsdp", axis=0, tiled=True),
        lax.all_gather(ffn_post_norm, "fsdp", axis=0, tiled=True),
    )
    unused, post_ffn_back = jax.vjp(rms_gain, down_out, g_ffn_post_gain)
    d_down, d_ffn_post = post_ffn_back(grad_out)
    d_down_low = d_down.astype(bf16)
    grad_w_down = jnp.einsum("tf,td->fd", mixed_low, d_down_low, preferred_element_type=f32)
    d_mixed = jnp.einsum("td,fd->tf", d_down_low, wd_full, preferred_element_type=f32)
    unused, glu_back = jax.vjp(gated_gelu, gate_proj, up_proj)
    d_gate, d_up = glu_back(d_mixed)
    d_gate_low = d_gate.astype(bf16)
    d_up_low = d_up.astype(bf16)
    grad_w_gate = jnp.einsum("td,tf->df", ffn_in, d_gate_low, preferred_element_type=f32)
    grad_w_up = jnp.einsum("td,tf->df", ffn_in, d_up_low, preferred_element_type=f32)
    d_ffn_in = jnp.einsum(
        "tf,df->td", d_gate_low, wg_full, preferred_element_type=f32
    ) + jnp.einsum("tf,df->td", d_up_low, wu_full, preferred_element_type=f32)
    unused, ffn_norm_back = jax.vjp(rms_gain, hidden_res, g_ffn_gain)
    d_hidden_part, d_ffn_norm = ffn_norm_back(d_ffn_in)
    d_hidden = grad_out + d_hidden_part
    ffn_sums = (
        lax.psum_scatter(d_ffn_norm, "fsdp", scatter_dimension=0, tiled=True),
        lax.psum_scatter(grad_w_gate, "fsdp", scatter_dimension=0, tiled=True),
        lax.psum_scatter(grad_w_up, "fsdp", scatter_dimension=0, tiled=True),
        lax.psum_scatter(grad_w_down, "fsdp", scatter_dimension=0, tiled=True),
        lax.psum_scatter(d_ffn_post, "fsdp", scatter_dimension=0, tiled=True),
    )
    g_attn, wq_full, wk_full, wv_full, gq_full, gk_full, wo_full, g_attn_post = (
        lax.all_gather(attn_norm, "fsdp", axis=0, tiled=True),
        lax.all_gather(w_query, "fsdp", axis=0, tiled=True),
        lax.all_gather(w_key, "fsdp", axis=0, tiled=True),
        lax.all_gather(w_value, "fsdp", axis=0, tiled=True),
        lax.all_gather(query_norm, "fsdp", axis=0, tiled=True),
        lax.all_gather(key_norm, "fsdp", axis=0, tiled=True),
        lax.all_gather(w_output, "fsdp", axis=0, tiled=True),
        lax.all_gather(attn_post_norm, "fsdp", axis=0, tiled=True),
    )
    unused, post_attn_back = jax.vjp(rms_gain, attn_branch, g_post_gain)
    d_branch, d_attn_post = post_attn_back(d_hidden)
    d_branch_low = d_branch.astype(bf16)
    grad_w_output = jnp.einsum("tc,td->cd", att_low, d_branch_low, preferred_element_type=f32)
    d_attended = (
        jnp.einsum("td,cd->tc", d_branch_low, wo_full, preferred_element_type=f32)
        .reshape(tok_rows, HQ, HD)
        .astype(bf16)
    )
    scores = masked_scores(q_low, key_rows, key_mask)
    prob_rows = jnp.exp(scores - log_total)
    prob_low = prob_rows.astype(bf16)
    d_values = jnp.einsum("htk,thd->kd", prob_low, d_attended, preferred_element_type=f32)
    d_probs = jnp.einsum("thd,kd->htk", d_attended, value_rows, preferred_element_type=f32)
    d_scores = prob_rows * (d_probs - jnp.sum(prob_rows * d_probs, axis=-1, keepdims=True))
    d_scores_low = d_scores.astype(bf16)
    d_queries = (
        jnp.einsum("htk,kd->thd", d_scores_low, key_rows, preferred_element_type=f32) * ATTN_SCALE
    )
    d_keys = jnp.einsum("htk,thd->kd", d_scores_low, q_low, preferred_element_type=f32) * ATTN_SCALE
    own_keys = d_keys[halo_count * tok_rows :]
    own_values = d_values[halo_count * tok_rows :]
    for distance in range(halo_count, 0, -1):
        part_index = halo_count - distance
        back_keys, back_values = shifted_2(
            (
                d_keys[part_index * tok_rows : (part_index + 1) * tok_rows],
                d_values[part_index * tok_rows : (part_index + 1) * tok_rows],
            ),
            "ctx",
            -distance,
        )
        own_keys = own_keys + back_keys
        own_values = own_values + back_values
    unused, turn_back = jax.vjp(
        lambda q_in, k_in, gq_in, gk_in: query_key(q_in, k_in, gq_in, gk_in, cosine, sine_table),
        q_pre,
        k_pre,
        gq_gain,
        gk_gain,
    )
    d_q_pre, d_k_pre, d_query_norm, d_key_norm = turn_back(
        (d_queries, own_keys.reshape(tok_rows, 1, HD))
    )
    dq_low = d_q_pre.reshape(tok_rows, HQ * HD).astype(bf16)
    dk_low = d_k_pre.reshape(tok_rows, HD).astype(bf16)
    dv_low = own_values.astype(bf16)
    grad_w_query = jnp.einsum("td,tc->dc", attn_in, dq_low, preferred_element_type=f32)
    grad_w_key = jnp.einsum("td,tc->dc", attn_in, dk_low, preferred_element_type=f32)
    grad_w_value = jnp.einsum("td,tc->dc", attn_in, dv_low, preferred_element_type=f32)
    d_attn_in = (
        jnp.einsum("tc,dc->td", dq_low, wq_full, preferred_element_type=f32)
        + jnp.einsum("tc,dc->td", dk_low, wk_full, preferred_element_type=f32)
        + jnp.einsum("tc,dc->td", dv_low, wv_full, preferred_element_type=f32)
    )
    unused, first_back = jax.vjp(rms_gain, inputs, g_attn.astype(f32))
    d_inputs_part, d_attn_norm = first_back(d_attn_in)
    d_tokens = d_hidden + d_inputs_part
    attn_sums = (
        lax.psum_scatter(d_attn_norm, "fsdp", scatter_dimension=0, tiled=True),
        lax.psum_scatter(grad_w_query, "fsdp", scatter_dimension=0, tiled=True),
        lax.psum_scatter(grad_w_key, "fsdp", scatter_dimension=0, tiled=True),
        lax.psum_scatter(grad_w_value, "fsdp", scatter_dimension=0, tiled=True),
        lax.psum_scatter(d_query_norm, "fsdp", scatter_dimension=0, tiled=True),
        lax.psum_scatter(d_key_norm, "fsdp", scatter_dimension=0, tiled=True),
        lax.psum_scatter(grad_w_output, "fsdp", scatter_dimension=0, tiled=True),
        lax.psum_scatter(d_attn_post, "fsdp", scatter_dimension=0, tiled=True),
    )
    column_sums = (
        lax.psum_scatter(attn_sums[1], "ctx", scatter_dimension=1, tiled=True),
        lax.psum_scatter(attn_sums[2], "ctx", scatter_dimension=1, tiled=True),
        lax.psum_scatter(attn_sums[3], "ctx", scatter_dimension=1, tiled=True),
        lax.psum_scatter(attn_sums[6], "ctx", scatter_dimension=1, tiled=True),
        lax.psum_scatter(ffn_sums[1], "ctx", scatter_dimension=1, tiled=True),
        lax.psum_scatter(ffn_sums[2], "ctx", scatter_dimension=1, tiled=True),
        lax.psum_scatter(ffn_sums[3], "ctx", scatter_dimension=1, tiled=True),
    )
    full_columns = (
        lax.all_gather(column_sums[0], "ctx", axis=1, tiled=True),
        lax.all_gather(column_sums[1], "ctx", axis=1, tiled=True),
        lax.all_gather(column_sums[2], "ctx", axis=1, tiled=True),
        lax.all_gather(column_sums[3], "ctx", axis=1, tiled=True),
        lax.all_gather(column_sums[4], "ctx", axis=1, tiled=True),
        lax.all_gather(column_sums[5], "ctx", axis=1, tiled=True),
        lax.all_gather(column_sums[6], "ctx", axis=1, tiled=True),
    )
    gain_totals = lax.psum(
        (attn_sums[0], attn_sums[4], attn_sums[5], attn_sums[7], ffn_sums[0], ffn_sums[4]), "ctx"
    )
    results = (
        gain_totals[0],
        full_columns[0],
        full_columns[1],
        full_columns[2],
        gain_totals[1],
        gain_totals[2],
        full_columns[3],
        gain_totals[3],
        gain_totals[4],
        full_columns[4],
        full_columns[5],
        full_columns[6],
        gain_totals[5],
    )
    out_rows = layer_out.astype(bf16).reshape(1, tok_rows, model_width)
    grad_rows = d_tokens.astype(bf16).reshape(1, tok_rows, model_width)
    return (
        out_rows,
        grad_rows,
        results[0],
        results[1],
        results[2],
        results[3],
        results[4],
        results[5],
        results[6],
        results[7],
        results[8],
        results[9],
        results[10],
        results[11],
        results[12],
    )


def solution(mesh):
    return jax.shard_map(
        body,
        mesh=mesh,
        in_specs=(
            P("fsdp", "ctx", None),
            P("fsdp", "ctx"),
            P("fsdp", "ctx", None),
            P("fsdp"),
            P("fsdp", None),
            P("fsdp", None),
            P("fsdp", None),
            P("fsdp"),
            P("fsdp"),
            P("fsdp", None),
            P("fsdp"),
            P("fsdp"),
            P("fsdp", None),
            P("fsdp", None),
            P("fsdp", None),
            P("fsdp"),
        ),
        out_specs=(
            P("fsdp", "ctx", None),
            P("fsdp", "ctx", None),
            P("fsdp"),
            P("fsdp", None),
            P("fsdp", None),
            P("fsdp", None),
            P("fsdp"),
            P("fsdp"),
            P("fsdp", None),
            P("fsdp"),
            P("fsdp"),
            P("fsdp", None),
            P("fsdp", None),
            P("fsdp", None),
            P("fsdp"),
        ),
        check_vma=False,
    )
```

profile of v0, /device:TPU:0, one launch (start us, length us, event | category | flops | bytes accessed | tf_op | source)
XLA Modules:
  0.0 1069.3 jit_solution(13079703393461077412)
XLA Ops:
  17.8 23.7 %all-reduce.18 = (bf16[640]{0:T(1024)(128)(2,1)S(1)}, bf16[256]{0:T(256)(128)(2,1)S(1)}, bf16[256]{0:T(256)(128)(2,1)S(1)}, bf16[640]{0:T(1024)(128)(2,1)S(1)}, ...) all-reduce(bf16[640]{0:T(1024)(128)(2,1)S(1)} %dynamic-update-slice, ...), channel_id=1, replica_groups=mesh['fsdp'=8,'ctx'=4] {'fsdp'}, use_global_device_ids=true, to_apply=%add.4 | all-reduce | flops 3072 | bytes 12288
  42.6 31.2 %all_gather.70 = bf16[640,256]{1,0:T(8,128)(2,1)S(1)} all-gather(bf16[80,256]{1,0:T(8,128)(2,1)} %param.21), channel_id=1, replica_groups=mesh['fsdp'=8,'ctx'=4] {'fsdp'}, dimensions={0}, use_global_device_ids=true | all-gather | bytes 368640 | tf_op jit(solution)/shard_map/all_gather | solution.py:94
  76.7 4.3 collective-permute-start.6
  83.0 31.5 %all_gather.69 = bf16[640,256]{1,0:T(8,128)(2,1)S(1)} all-gather(bf16[80,256]{1,0:T(8,128)(2,1)S(1)} %copy-done.35), channel_id=1, replica_groups=mesh['fsdp'=8,'ctx'=4] {'fsdp'}, dimensions={0}, use_global_device_ids=true | all-gather | bytes 368640 | tf_op jit(solution)/shard_map/all_gather | solution.py:95
  129.0 29.5 %all-gather.10.cloned.1.call-done = bf16[640,2048]{1,0:T(8,128)(2,1)} async-done(((bf16[80,2048]{1,0:T(8,128)(2,1)}), bf16[640,2048]{1,0:T(8,128)(2,1)}) %all-gather.10.cloned.1.call-update) | async-done | bytes 2621456 | tf_op jit(solution)/shard_map/all_gather | solution.py:143
  158.4 3.3 fusion.102
  161.7 52.0 %all-gather.12.cloned.1.call-done = bf16[640,2048]{1,0:T(8,128)(2,1)} async-done(((bf16[80,2048]{1,0:T(8,128)(2,1)}), bf16[640,2048]{1,0:T(8,128)(2,1)}) %all-gather.12.cloned.1.call-update) | async-done | bytes 2621456 | tf_op jit(solution)/shard_map/all_gather | solution.py:144
  213.7 3.8 multiply_convert_fusion.2
  217.5 51.5 %all-gather.14.cloned.1.call-done = bf16[2048,640]{1,0:T(8,128)(2,1)} async-done(((bf16[256,640]{1,0:T(8,128)(2,1)}), bf16[2048,640]{1,0:T(8,128)(2,1)}) %all-gather.14.cloned.1.call-update) | async-done | bytes 2621456 | tf_op jit(solution)/shard_map/all_gather | solution.py:145
  294.5 4.5 collective-permute-done.10
  310.0 3.3 fusion.107
  321.7 34.9 %reduce-scatter.29.cloned.1.call-done = f32[80,256]{1,0:T(8,128)} async-done(((f32[640,256]{1,0:T(8,128)}), f32[80,256]{1,0:T(8,128)}) %reduce-scatter.29.cloned.1.call-update) | async-done | bytes 81936 | tf_op jit(solution)/shard_map/reduce_scatter | solution.py:259
  358.2 63.6 %reduce-scatter.27.cloned.1.call-done = f32[80,256]{1,0:T(8,128)} async-done(((f32[640,256]{1,0:T(8,128)}), f32[80,256]{1,0:T(8,128)}) %reduce-scatter.27.cloned.1.call-update) | async-done | bytes 81936 | tf_op jit(solution)/shard_map/reduce_scatter | solution.py:258
  423.5 71.4 %reduce-scatter.31.cloned.1.call-done = f32[128,640]{1,0:T(8,128)} async-done(((f32[1024,640]{1,0:T(8,128)}), f32[128,640]{1,0:T(8,128)}) %reduce-scatter.31.cloned.1.call-update) | async-done | bytes 327696 | tf_op jit(solution)/shard_map/reduce_scatter | solution.py:262
  496.9 70.9 %reduce-scatter.23.cloned.1.call-done = f32[80,1024]{1,0:T(8,128)} async-done(((f32[640,1024]{1,0:T(8,128)}), f32[80,1024]{1,0:T(8,128)}) %reduce-scatter.23.cloned.1.call-update) | async-done | bytes 327696 | tf_op jit(solution)/shard_map/reduce_scatter | solution.py:257
  567.9 105.0 %reduce-scatter.37.cloned.1.call-done = f32[80,2048]{1,0:T(8,128)} async-done(((f32[640,2048]{1,0:T(8,128)}), f32[80,2048]{1,0:T(8,128)}) %reduce-scatter.37.cloned.1.call-update) | async-done | bytes 655376 | tf_op jit(solution)/shard_map/reduce_scatter | solution.py:183
  672.9 106.0 %reduce-scatter.33.cloned.1.call-done = f32[80,2048]{1,0:T(8,128)} async-done(((f32[640,2048]{1,0:T(8,128)}), f32[80,2048]{1,0:T(8,128)}) %reduce-scatter.33.cloned.1.call-update) | async-done | bytes 655376 | tf_op jit(solution)/shard_map/reduce_scatter | solution.py:182
  781.2 103.7 %reduce-scatter.41.cloned.1.call-done = f32[256,640]{1,0:T(8,128)} async-done(((f32[2048,640]{1,0:T(8,128)}), f32[256,640]{1,0:T(8,128)}) %reduce-scatter.41.cloned.1.call-update) | async-done | bytes 655376 | tf_op jit(solution)/shard_map/reduce_scatter | solution.py:184
  887.5 35.9 %all-reduce.16 = (f32[640]{0:T(1024)S(1)}, f32[256]{0:T(256)S(1)}, f32[256]{0:T(256)S(1)}, f32[640]{0:T(1024)S(1)}, f32[640]{0:T(1024)S(1)}, /*index=5*/f32[640]{0:T(1024)S(1)}) all-reduce(f32[640]{0:T(1024)S(1)} %get-tuple-element.38, f32[256]{0:T(256)S(1)} %get-tuple-element.30, ...), channel_id=2, replica_groups=mesh['fsdp'=8,'ctx'=4] {'fsdp'}, use_global_device_ids=true, to_apply=%region_16.17.clone | all-reduce | flops 3072 | bytes 24576
  923.9 6.6 all-reduce.17
  931.3 5.6 all_gather.83
  937.6 5.6 all_gather.82
  944.0 9.4 reduce-scatter.47.cloned.1.call-done
  953.3 6.2 all_gather.84
  960.4 15.9 %reduce-scatter.25.cloned.1.call-done = f32[80,256]{1,0:T(8,128)} async-done(((f32[80,1024]{1,0:T(8,128)}), f32[80,256]{1,0:T(8,128)}) %reduce-scatter.25.cloned.1.call-update) | async-done | bytes 81936 | tf_op jit(solution)/shard_map/reduce_scatter | solution.py:266
  976.3 6.2 all_gather.81
  982.5 18.7 %reduce-scatter.39.cloned.1.call-done = f32[80,512]{1,0:T(8,128)} async-done(((f32[80,2048]{1,0:T(8,128)}), f32[80,512]{1,0:T(8,128)}) %reduce-scatter.39.cloned.1.call-update) | async-done | bytes 163856 | tf_op jit(solution)/shard_map/reduce_scatter | solution.py:271
  1001.2 7.7 all_gather.86
  1008.8 17.2 %reduce-scatter.35.cloned.1.call-done = f32[80,512]{1,0:T(8,128)} async-done(((f32[80,2048]{1,0:T(8,128)}), f32[80,512]{1,0:T(8,128)}) %reduce-scatter.35.cloned.1.call-update) | async-done | bytes 163856 | tf_op jit(solution)/shard_map/reduce_scatter | solution.py:270
  1026.0 7.7 all_gather.85
  1033.7 17.9 %reduce-scatter.49.cloned.1.call-done = f32[160,256]{1,0:T(8,128)} async-done(((f32[640,256]{1,0:T(8,128)}), f32[160,256]{1,0:T(8,128)}) %reduce-scatter.49.cloned.1.call-update) | async-done | bytes 163856
  1051.6 7.7 all_gather.87
  (324 shorter events, 89.1 us)
Async XLA Ops:
  7.2 114.9 %all-gather.6.cloned.1.call-start = ((), (), s32[]{:S(2)}) async-start(), calls=%async_computation.14 | async-start | bytes 1474560 | tf_op jit(solution)/shard_map/all_gather | solution.py:93
  7.9 118.1 %all-gather.8.cloned.1.call-start = ((), (), s32[]{:S(2)}) async-start(), calls=%async_computation.15 | async-start | bytes 1474560 | tf_op jit(solution)/shard_map/all_gather | solution.py:98
  8.7 149.7 %all-gather.10.cloned.1.call-start = ((), (), s32[]{:S(2)}) async-start(), calls=%async_computation.16 | async-start | bytes 2949120 | tf_op jit(solution)/shard_map/all_gather | solution.py:143
  9.4 204.3 %all-gather.12.cloned.1.call-start = ((), (), s32[]{:S(2)}) async-start(), calls=%async_computation.17 | async-start | bytes 2949120 | tf_op jit(solution)/shard_map/all_gather | solution.py:144
  10.0 259.0 %all-gather.14.cloned.1.call-start = ((), (), s32[]{:S(2)}) async-start(), calls=%async_computation.18 | async-start | bytes 2949120 | tf_op jit(solution)/shard_map/all_gather | solution.py:145
  75.4 45.7 %collective-permute-start.7 = (bf16[128,256]{1,0:T(8,128)(2,1)S(1)}, bf16[128,256]{1,0:T(8,128)(2,1)S(1)}, u32[]{:S(2)}, u32[]{:S(2)}) collective-permute-start(bf16[128,256]{1,0:T(8,128)(2,1)S(1)} %maximum_bitcast_fusion), channel_id=1, source_target_pairs={{0,1},{1,2},{2,3},{4,5},{5,6},{6,7},{8,9},{9,10},{10,11},{12,13},{... | collective-permute-start | bytes 196616 | tf_op jit(solution)/shard_map/ppermute | solution.py:19
  76.7 43.5 %collective-permute-start.6 = (bf16[128,256]{1,0:T(8,128)(2,1)S(1)}, bf16[128,256]{1,0:T(8,128)(2,1)S(1)}, u32[]{:S(2)}, u32[]{:S(2)}) collective-permute-start(bf16[128,256]{1,0:T(8,128)(2,1)S(1)} %maximum_bitcast_fusion), channel_id=1, source_target_pairs={{0,2},{1,3},{4,6},{5,7},{8,10},{9,11},{12,14},{13,15},{16,18},{17,... | collective-permute-start | bytes 196616 | tf_op jit(solution)/shard_map/ppermute | solution.py:19
  81.0 37.9 %collective-permute-start.5 = (bf16[128,256]{1,0:T(8,128)(2,1)S(1)}, bf16[128,256]{1,0:T(8,128)(2,1)S(1)}, u32[]{:S(2)}, u32[]{:S(2)}) collective-permute-start(bf16[128,256]{1,0:T(8,128)(2,1)S(1)} %maximum_bitcast_fusion), channel_id=1, source_target_pairs={{0,3},{4,7},{8,11},{12,15},{16,19},{20,23},{24,27},{28,31}} | collective-permute-start | bytes 196616 | tf_op jit(solution)/shard_map/ppermute | solution.py:19
  82.3 35.2 %collective-permute-start.4 = (bf16[128,256]{1,0:T(8,128)(2,1)S(1)}, bf16[128,256]{1,0:T(8,128)(2,1)S(1)}, u32[]{:S(2)}, u32[]{:S(2)}) collective-permute-start(bf16[128,256]{1,0:T(8,128)(2,1)S(1)} %maximum_bitcast_fusion), channel_id=1, source_target_pairs={} | collective-permute-start | bytes 196616 | tf_op jit(solution)/shard_map/ppermute | solution.py:19
  115.5 6.6 collective-permute-start.3
  116.8 239.7 %reduce-scatter.29.cloned.1.call-start = ((), (), s32[]{:S(2)}) async-start(), calls=%async_computation.22 | async-start | bytes 737280 | tf_op jit(solution)/shard_map/reduce_scatter | solution.py:259
  281.5 7.3 collective-permute-start.12
  282.2 7.9 collective-permute-start.15
  283.5 8.1 collective-permute-start.14
  284.8 8.4 collective-permute-start.13
  288.1 6.4 collective-permute-start.8
  288.8 5.7 collective-permute-start.11
  290.1 8.9 collective-permute-start.10
  291.6 8.6 collective-permute-start.9
  294.5 127.3 %reduce-scatter.27.cloned.1.call-start = ((), (), s32[]{:S(2)}) async-start(), calls=%async_computation.21 | async-start | bytes 737280 | tf_op jit(solution)/shard_map/reduce_scatter | solution.py:258
  302.1 192.8 %reduce-scatter.31.cloned.1.call-start = ((), (), s32[]{:S(2)}) async-start(), calls=%async_computation.23 | async-start | bytes 2949120 | tf_op jit(solution)/shard_map/reduce_scatter | solution.py:262
  304.2 263.6 %reduce-scatter.23.cloned.1.call-start = ((), (), s32[]{:S(2)}) async-start(), calls=%async_computation.19 | async-start | bytes 2949120 | tf_op jit(solution)/shard_map/reduce_scatter | solution.py:257
  309.0 363.8 %reduce-scatter.37.cloned.1.call-start = ((), (), s32[]{:S(2)}) async-start(), calls=%async_computation.26 | async-start | bytes 5898240 | tf_op jit(solution)/shard_map/reduce_scatter | solution.py:183
  313.3 465.7 %reduce-scatter.33.cloned.1.call-start = ((), (), s32[]{:S(2)}) async-start(), calls=%async_computation.24 | async-start | bytes 5898240 | tf_op jit(solution)/shard_map/reduce_scatter | solution.py:182
  317.5 567.4 %reduce-scatter.41.cloned.1.call-start = ((), (), s32[]{:S(2)}) async-start(), calls=%async_computation.28 | async-start | bytes 5898240 | tf_op jit(solution)/shard_map/reduce_scatter | solution.py:184
  321.6 609.7 %reduce-scatter.45.cloned.1.call-start = ((), (), s32[]{:S(2)}) async-start(), calls=%async_computation.30 | async-start | bytes 163840
  358.2 579.4 %reduce-scatter.43.cloned.1.call-start = ((), (), s32[]{:S(2)}) async-start(), calls=%async_computation.29 | async-start | bytes 163840
  423.5 529.8 %reduce-scatter.47.cloned.1.call-start = ((), (), s32[]{:S(2)}) async-start(), calls=%async_computation.31 | async-start | bytes 409600
  496.8 479.5 %reduce-scatter.25.cloned.1.call-start = ((), (), s32[]{:S(2)}) async-start(), calls=%async_computation.20 | async-start | bytes 409600 | tf_op jit(solution)/shard_map/reduce_scatter | solution.py:266
  567.9 433.3 %reduce-scatter.39.cloned.1.call-start = ((), (), s32[]{:S(2)}) async-start(), calls=%async_computation.27 | async-start | bytes 819200 | tf_op jit(solution)/shard_map/reduce_scatter | solution.py:271
  672.9 353.1 %reduce-scatter.35.cloned.1.call-start = ((), (), s32[]{:S(2)}) async-start(), calls=%async_computation.25 | async-start | bytes 819200 | tf_op jit(solution)/shard_map/reduce_scatter | solution.py:270
  779.0 272.6 %reduce-scatter.49.cloned.1.call-start = ((), (), s32[]{:S(2)}) async-start(), calls=%async_computation.32 | async-start | bytes 819200
  (71 other events, 1776.4 us)
Sparse Core Ops, SparseCore 0:
  10.2 46.6 all-gather.5
  59.1 44.3 all-gather.7
  105.7 52.6 all-gather.9
  160.5 53.2 all-gather.11
  215.8 53.2 all-gather.13
  294.6 61.8 reduce-scatter.28
  360.7 61.0 reduce-scatter.26
  425.3 69.6 reduce-scatter.30
  498.5 69.3 reduce-scatter.22
  571.3 101.5 reduce-scatter.36
  676.4 102.4 reduce-scatter.32
  782.4 102.4 reduce-scatter.40
  887.9 19.3 reduce-scatter.44
  910.3 19.5 reduce-scatter.42
  932.8 20.4 reduce-scatter.46
  955.8 20.4 reduce-scatter.24
  978.7 22.4 reduce-scatter.38
  1003.5 22.4 reduce-scatter.34
  1029.1 22.4 reduce-scatter.48
where the time goes:
time: 1070 us
  waiting for transfers between devices  777 us (73%)
  blocking collectives  175 us (16%)
  matrix products  36.2 us (3%)
  local copies, waits for them, and re-layouts  31.6 us (3%)
  starting transfers between devices  22.4 us (2%)
  between operations  18 us (2%)
    reduce_scatter x1, waiting for transfers between devices, body(): lax.psum_scatter(grad_w_gate, 'fsdp', scatter_dimension=0, tiled=True)  106 us
    reduce_scatter x1, waiting for transfers between devices, body(): lax.psum_scatter(grad_w_up, 'fsdp', scatter_dimension=0, tiled=True)  105 us
    reduce_scatter x1, waiting for transfers between devices, body(): lax.psum_scatter(grad_w_down, 'fsdp', scatter_dimension=0, tiled=True)  104 us
    reduce_scatter x1, waiting for transfers between devices, body(): lax.psum_scatter(grad_w_output, 'fsdp', scatter_dimension=0, tiled=True)  71.4 us
    reduce_scatter x1, waiting for transfers between devices, body(): lax.psum_scatter(grad_w_query, 'fsdp', scatter_dimension=0, tiled=True)  70.9 us
    reduce_scatter x1, waiting for transfers between devices, body(): lax.psum_scatter(grad_w_key, 'fsdp', scatter_dimension=0, tiled=True)  63.6 us
    unnamed x2, blocking collectives  59.7 us
    all_gather x1, waiting for transfers between devices, body(): lax.all_gather(w_up, 'fsdp', axis=0, tiled=True)  52 us
  transfers between devices with their start and end apart: 35, of which 20 were waited for; matrix products, arithmetic and copies ran while one was open for 5% of the time, Pallas kernels for 0%

commit v1 on v0

--- a/solution.py
+++ b/solution.py
@@ -1,6 +1,10 @@
+import functools
+
 import jax
 import jax.numpy as jnp
 from jax import lax
+from jax.experimental import pallas as pl
+from jax.experimental.pallas import tpu as pltpu
 from jax.sharding import PartitionSpec as P
 
 HQ = 4
@@ -63,7 +67,7 @@
     return jnp.where(key_mask[None], raw_scores, NEGATIVE)
 
 
-def body(
+def plain_body(
     tokens,
     positions,
     cotangent,
@@ -319,9 +323,459 @@
     )
 
 
+VMEM_BYTES = 48 * 1024 * 1024
+
+
+def peer_of(axis, index):
+    return dict(device_id={axis: index}, device_id_type=pl.DeviceIdType.MESH)
+
+
+def greet(axis, indices):
+    barrier = pltpu.get_barrier_semaphore()
+    for index in indices:
+        pl.semaphore_signal(barrier, inc=1, **peer_of(axis, index))
+    pl.semaphore_wait(barrier, len(indices))
+
+
+def gather_kernel(axis, n, count, *refs):
+    ins, outs = refs[:count], refs[count : 2 * count]
+    send, recv = refs[2 * count :]
+    me = lax.axis_index(axis)
+    outer, inner = lax.div(me, 2), lax.rem(me, 2)
+    span = n // 2
+    twin = outer * 2 + (1 - inner)
+
+    def ahead(step):
+        return lax.rem(outer + step, span) * 2 + inner
+
+    def behind(step):
+        return lax.rem(outer + span - step, span)
+
+    greet(axis, [twin] + [ahead(step) for step in range(1, span)])
+
+    def copy(i, source, slot, lane, target):
+        return pltpu.make_async_remote_copy(
+            src_ref=source,
+            dst_ref=outs[i].at[slot],
+            send_sem=send.at[i, lane],
+            recv_sem=recv.at[i, lane],
+            **peer_of(axis, target),
+        )
+
+    for i in range(count):
+        for step in range(1, span):
+            copy(i, ins[i], me, step, ahead(step)).start()
+        copy(i, ins[i], me, 0, twin).start()
+    for i in range(count):
+        outs[i][me] = ins[i][...]
+    for i in range(count):
+        for step in range(1, span):
+            slot = behind(step) * 2 + inner
+            copy(i, ins[i], slot, step, twin).wait_recv()
+            copy(i, outs[i].at[slot], slot, span - 1 + step, twin).start()
+    for i in range(count):
+        copy(i, ins[i], twin, 0, twin).wait_recv()
+        for step in range(1, span):
+            slot = behind(step) * 2 + (1 - inner)
+            copy(i, ins[i], slot, span - 1 + step, twin).wait_recv()
+        for lane in range(2 * span - 1):
+            copy(i, ins[i], me, lane, twin).wait_send()
+
+
+def gather(axis, n, key, *arrays):
+    count = len(arrays)
+    spec = pl.BlockSpec(memory_space=pltpu.VMEM)
+    return pl.pallas_call(
+        functools.partial(gather_kernel, axis, n, count),
+        out_shape=[jax.ShapeDtypeStruct((n,) + a.shape, a.dtype) for a in arrays],
+        in_specs=[spec] * count,
+        out_specs=[spec] * count,
+        scratch_shapes=[
+            pltpu.SemaphoreType.DMA((count, n - 1)),
+            pltpu.SemaphoreType.DMA((count, n - 1)),
+        ],
+        compiler_params=pltpu.CompilerParams(
+            collective_id=key, has_side_effects=True, vmem_limit_bytes=VMEM_BYTES
+        ),
+    )(*arrays)
+
+
+def add_scatter_kernel(axis, n, count, *refs):
+    ins, outs = refs[:count], refs[count : 2 * count]
+    from_twin, paired, landed = (
+        refs[2 * count : 3 * count],
+        refs[3 * count : 4 * count],
+        refs[4 * count : 5 * count],
+    )
+    send, recv = refs[5 * count :]
+    me = lax.axis_index(axis)
+    outer, inner = lax.div(me, 2), lax.rem(me, 2)
+    span = n // 2
+    twin = outer * 2 + (1 - inner)
+    f32 = jnp.float32
+
+    def ahead(step):
+        return lax.rem(outer + step, span)
+
+    greet(axis, [twin] + [ahead(step) * 2 + inner for step in range(1, span)])
+
+    def to_twin(i, step):
+        return pltpu.make_async_remote_copy(
+            src_ref=ins[i].at[ahead(step) * 2 + (1 - inner)],
+            dst_ref=from_twin[i].at[step],
+            send_sem=send.at[i, step],
+            recv_sem=recv.at[i, step],
+            **peer_of(axis, twin),
+        )
+
+    def to_owner(i, step):
+        return pltpu.make_async_remote_copy(
+            src_ref=paired[i].at[step],
+            dst_ref=landed[i].at[step],
+            send_sem=send.at[i, span + step],
+            recv_sem=recv.at[i, span + step],
+            **peer_of(axis, ahead(step) * 2 + inner),
+        )
+
+    order = list(range(1, span)) + [0]
+    for i in range(count):
+        for step in order:
+            to_twin(i, step).start()
+    for i in range(count):
+        for step in range(1, span):
+            to_twin(i, step).wait_recv()
+            paired[i][step] = (
+                ins[i][ahead(step) * 2 + inner].astype(f32) + from_twin[i][step].astype(f32)
+            ).astype(paired[i].dtype)
+            to_owner(i, step).start()
+    for i in range(count):
+        to_twin(i, 0).wait_recv()
+        total = ins[i][me].astype(f32) + from_twin[i][0].astype(f32)
+        for step in range(1, span):
+            to_owner(i, step).wait_recv()
+            total = total + landed[i][step].astype(f32)
+        outs[i][...] = total.astype(outs[i].dtype)
+    for i in range(count):
+        for step in range(span):
+            to_twin(i, step).wait_send()
+        for step in range(1, span):
+            to_owner(i, step).wait_send()
+
+
+def add_scatter(axis, n, key, out_type, *arrays):
+    count = len(arrays)
+    spec = pl.BlockSpec(memory_space=pltpu.VMEM)
+    slots = [pltpu.VMEM((n // 2,) + a.shape[1:], a.dtype) for a in arrays]
+    return pl.pallas_call(
+        functools.partial(add_scatter_kernel, axis, n, count),
+        out_shape=[jax.ShapeDtypeStruct(a.shape[1:], out_type) for a in arrays],
+        in_specs=[spec] * count,
+        out_specs=[spec] * count,
+        scratch_shapes=slots * 3
+        + [
+            pltpu.SemaphoreType.DMA((count, n)),
+            pltpu.SemaphoreType.DMA((count, n)),
+        ],
+        compiler_params=pltpu.CompilerParams(
+            collective_id=key, has_side_effects=True, vmem_limit_bytes=VMEM_BYTES
+        ),
+    )(*arrays)
+
+
+def swap_kernel(axis, n, in_ref, out_ref, send, recv):
+    me = lax.axis_index(axis)
+
+    def ahead(step):
+        return lax.rem(me + step, n)
+
+    greet(axis, [ahead(step) for step in range(1, n)])
+
+    def copy(step, slot):
+        return pltpu.make_async_remote_copy(
+            src_ref=in_ref.at[ahead(step)],
+            dst_ref=out_ref.at[slot],
+            send_sem=send.at[step],
+            recv_sem=recv.at[step],
+            **peer_of(axis, ahead(step)),
+        )
+
+    for step in range(1, n):
+        copy(step, me).start()
+    out_ref[me] = in_ref[me]
+    for step in range(1, n):
+        copy(step, lax.rem(me + n - step, n)).wait_recv()
+    for step in range(1, n):
+        copy(step, me).wait_send()
+
+
+def swap(axis, n, key, array):
+    spec = pl.BlockSpec(memory_space=pltpu.VMEM)
+    return pl.pallas_call(
+        functools.partial(swap_kernel, axis, n),
+        out_shape=jax.ShapeDtypeStruct(array.shape, array.dtype),
+        in_specs=[spec],
+        out_specs=spec,
+        scratch_shapes=[pltpu.SemaphoreType.DMA((n,)), pltpu.SemaphoreType.DMA((n,))],
+        compiler_params=pltpu.CompilerParams(
+            collective_id=key, has_side_effects=True, vmem_limit_bytes=VMEM_BYTES
+        ),
+    )(array)
+
+
+def turned_norm(values, gain_vec, cosine, sine_table):
+    return rotate(rms_gain(values, gain_vec), cosine, sine_table)
+
+
+def split_body(
+    tokens,
+    positions,
+    cotangent,
+    attn_norm,
+    w_query,
+    w_key,
+    w_value,
+    query_norm,
+    key_norm,
+    w_output,
+    attn_post_norm,
+    ffn_norm,
+    w_gate,
+    w_up,
+    w_down,
+    ffn_post_norm,
+):
+    f32 = jnp.float32
+    bf16 = jnp.bfloat16
+    ways = lax.axis_size("ctx")
+    owners = lax.axis_size("fsdp")
+    part = lax.axis_index("ctx")
+    rows, width = tokens.shape[1:]
+    seq = rows * ways
+    shard = w_query.shape[0]
+    hidden_row = w_down.shape[0] // ways
+    out_row = w_output.shape[0] // ways
+    head_share = query_norm.shape[0]
+    inputs = tokens.reshape(rows, width).astype(f32)
+    grad_out = cotangent.reshape(rows, width).astype(f32)
+
+    def mul(left, right, dims):
+        return lax.dot_general(left, right, (dims, ((), ())), preferred_element_type=f32)
+
+    def nn(left, right):
+        return mul(left, right, ((1,), (0,)))
+
+    def nt(left, right):
+        return mul(left, right, ((1,), (1,)))
+
+    def tn(left, right):
+        return mul(left, right, ((0,), (0,)))
+
+    def hidden_part(weight):
+        cut = weight.reshape(shard, owners, ways, hidden_row)
+        return lax.dynamic_index_in_dim(cut, part, 2, keepdims=False).reshape(
+            shard, owners * hidden_row
+        )
+
+    def hidden_whole(parts):
+        return (
+            parts.reshape(ways, shard, owners, hidden_row)
+            .transpose(1, 2, 0, 3)
+            .reshape(shard, owners * ways * hidden_row)
+        )
+
+    gain_row = jnp.concatenate(
+        [attn_norm, attn_post_norm, ffn_norm, ffn_post_norm, query_norm, key_norm]
+    )
+    gain_size = gain_row.shape[0]
+    attn_pack = jnp.concatenate(
+        [
+            jnp.concatenate(
+                [lax.dynamic_slice_in_dim(w_query, part * HD, HD, 1), w_key, w_value], axis=1
+            ),
+            jnp.pad(gain_row[None], ((0, 15), (0, 3 * HD - gain_size))),
+        ],
+        axis=0,
+    )
+    attn_all, wo_rows, wg_all, wu_all, wd_all = gather(
+        "fsdp",
+        owners,
+        0,
+        attn_pack,
+        lax.dynamic_slice_in_dim(w_output, part * out_row, out_row, 0),
+        hidden_part(w_gate),
+        hidden_part(w_up),
+        lax.dynamic_slice_in_dim(w_down, part * hidden_row, hidden_row, 0),
+    )
+    gains = attn_all[:, shard, :gain_size].astype(f32)
+
+    def gain_of(index):
+        return gains[:, index * shard : (index + 1) * shard].reshape(width)
+
+    g_attn, g_post, g_ffn, g_ffn_post = (gain_of(index) for index in range(4))
+    g_query = gains[:, 4 * shard : 4 * shard + head_share].reshape(HD)
+    g_key = gains[:, 4 * shard + head_share :].reshape(HD)
+    w_qkv = attn_all[:, :shard].reshape(width, 3 * HD)
+    wq_head, wk_full, wv_full = (w_qkv[:, i * HD : (i + 1) * HD] for i in range(3))
+    wg_part = wg_all.reshape(width, owners * hidden_row)
+    wu_part = wu_all.reshape(width, owners * hidden_row)
+    wd_part = wd_all.reshape(owners * hidden_row, width)
+    wo_head = (
+        swap("ctx", ways, 1, wo_rows.reshape(ways, owners // ways * out_row, width))
+        .reshape(ways, owners // ways, out_row, width)
+        .transpose(1, 0, 2, 3)
+        .reshape(HD, width)
+    )
+
+    attn_in = rms_gain(inputs, g_attn).astype(bf16)
+    attn_seq, place_all = gather(
+        "ctx", ways, 2, attn_in, jnp.broadcast_to(positions.reshape(1, rows), (8, rows))
+    )
+    attn_seq = attn_seq.reshape(seq, width)
+    seq_place = place_all[:, 0].reshape(seq)
+    index = jnp.arange(seq, dtype=jnp.int32)
+    key_mask = (
+        (index[None, :] <= index[:, None])
+        & (index[:, None] - index[None, :] < WINDOW)
+        & (index[None, :] >= (index - seq_place)[:, None])
+    )
+    cosine, sine_table = rope_tables(seq_place)
+    cosine, sine_table = cosine[:, 0], sine_table[:, 0]
+    qkv = nn(attn_seq, w_qkv)
+    q_pre, k_pre, v_pre = (qkv[:, i * HD : (i + 1) * HD] for i in range(3))
+    v_low = v_pre.astype(bf16)
+    q_low = turned_norm(q_pre, g_query, cosine, sine_table).astype(bf16)
+    k_low = turned_norm(k_pre, g_key, cosine, sine_table).astype(bf16)
+    scores = jnp.where(key_mask, nt(q_low, k_low) * ATTN_SCALE, NEGATIVE)
+    shifted = jnp.exp(scores - jnp.max(scores, axis=-1, keepdims=True))
+    prob_rows = shifted / jnp.sum(shifted, axis=-1, keepdims=True)
+    prob_low = prob_rows.astype(bf16)
+    att_low = nn(prob_low, v_low).astype(bf16)
+
+    def own_sum(key, value):
+        return add_scatter(
+            "ctx", ways, key, f32, value.astype(bf16).reshape(ways, rows, value.shape[1])
+        )[0]
+
+    def whole(key, value):
+        return gather("ctx", ways, key, value)[0].reshape(seq, value.shape[1])
+
+    branch = own_sum(3, nn(att_low, wo_head))
+    hidden_res = inputs + rms_gain(branch, g_post)
+    ffn_seq = whole(4, rms_gain(hidden_res, g_ffn).astype(bf16))
+    gate_proj = nn(ffn_seq, wg_part)
+    up_proj = nn(ffn_seq, wu_part)
+    mixed_low = gated_gelu(gate_proj, up_proj).astype(bf16)
+    down_out = own_sum(5, nn(mixed_low, wd_part))
+    layer_out = hidden_res + rms_gain(down_out, g_ffn_post)
+
+    d_down, d_ffn_post = jax.vjp(rms_gain, down_out, g_ffn_post)[1](grad_out)
+    d_down_seq = whole(6, d_down.astype(bf16))
+    d_mixed = nt(d_down_seq, wd_part)
+    d_gate, d_up = jax.vjp(gated_gelu, gate_proj, up_proj)[1](d_mixed)
+    d_gate_low = d_gate.astype(bf16)
+    d_up_low = d_up.astype(bf16)
+    d_ffn_in = own_sum(7, nt(d_gate_low, wg_part) + nt(d_up_low, wu_part))
+    grad_w_down = tn(mixed_low, d_down_seq)
+    grad_w_gate = tn(ffn_seq, d_gate_low)
+    grad_w_up = tn(ffn_seq, d_up_low)
+    d_hidden_part, d_ffn_norm = jax.vjp(rms_gain, hidden_res, g_ffn)[1](d_ffn_in)
+    d_hidden = grad_out + d_hidden_part
+
+    d_branch, d_post = jax.vjp(rms_gain, branch, g_post)[1](d_hidden)
+    d_branch_seq = whole(8, d_branch.astype(bf16))
+    grad_w_output = tn(att_low, d_branch_seq)
+    d_att = nt(d_branch_seq, wo_head).astype(bf16)
+    d_values = tn(prob_low, d_att)
+    d_probs = nt(d_att, v_low)
+    d_scores = prob_rows * (d_probs - jnp.sum(prob_rows * d_probs, axis=-1, keepdims=True))
+    d_scores_low = d_scores.astype(bf16)
+    d_queries = nn(d_scores_low, k_low) * ATTN_SCALE
+    d_keys = tn(d_scores_low, q_low) * ATTN_SCALE
+    d_q_pre, d_query_norm = jax.vjp(
+        lambda values, gain_vec: turned_norm(values, gain_vec, cosine, sine_table), q_pre, g_query
+    )[1](d_queries)
+    dq_low = d_q_pre.astype(bf16)
+    sums = own_sum(9, jnp.concatenate([nt(dq_low, wq_head), d_keys, d_values], axis=1))
+    own_cos = lax.dynamic_slice_in_dim(cosine, part * rows, rows, 0)
+    own_sin = lax.dynamic_slice_in_dim(sine_table, part * rows, rows, 0)
+    own_k = lax.dynamic_slice_in_dim(k_pre, part * rows, rows, 0)
+    d_k_pre, d_key_norm = jax.vjp(
+        lambda values, gain_vec: turned_norm(values, gain_vec, own_cos, own_sin), own_k, g_key
+    )[1](sums[:, width : width + HD])
+    dkv_low = jnp.concatenate([d_k_pre, sums[:, width + HD :]], axis=1).astype(bf16)
+    d_attn_in = sums[:, :width] + nt(dkv_low, w_qkv[:, HD:])
+    dkv_seq = whole(10, dkv_low)
+    d_inputs_part, d_attn_norm = jax.vjp(rms_gain, inputs, g_attn)[1](d_attn_in)
+    d_tokens = d_hidden + d_inputs_part
+    grad_w_query = tn(attn_seq, dq_low)
+    dkv_cols = 2 * HD // ways
+    grad_w_kv = tn(attn_seq, lax.dynamic_slice_in_dim(dkv_seq, part * dkv_cols, dkv_cols, 1))
+
+    grad_wo_rows = swap(
+        "ctx",
+        ways,
+        11,
+        grad_w_output.astype(bf16)
+        .reshape(owners // ways, ways, out_row, width)
+        .transpose(1, 0, 2, 3)
+        .reshape(ways, owners // ways * out_row, width),
+    ).reshape(owners, out_row, width)
+    gain_grads = jnp.concatenate(
+        [
+            value.reshape(owners, -1)
+            for value in (d_attn_norm, d_post, d_ffn_norm, d_ffn_post, d_query_norm, d_key_norm)
+        ],
+        axis=1,
+    )
+    gain_grads = jnp.pad(gain_grads[:, None], ((0, 0), (0, 15), (0, 0)))
+
+    def blocks(value):
+        return value.astype(bf16).reshape(owners, value.shape[0] // owners, value.shape[1])
+
+    mine = add_scatter(
+        "fsdp",
+        owners,
+        12,
+        bf16,
+        blocks(grad_w_gate),
+        blocks(grad_w_up),
+        blocks(grad_w_down),
+        blocks(grad_w_query),
+        grad_wo_rows,
+        blocks(grad_w_kv),
+        gain_grads.astype(bf16),
+    )
+    wg_g, wu_g, wd_g, wq_g, wo_g, wkv_g, gain_g = gather("ctx", ways, 13, *mine)
+    gain_sum = jnp.sum(gain_g[:, 0].astype(f32), axis=0)
+    ends = [shard * i for i in range(1, 5)] + [4 * shard + head_share]
+    t_attn, t_post, t_ffn, t_ffn_post, t_query, t_key = jnp.split(gain_sum, ends)
+    half = ways // 2
+
+    def columns(parts):
+        return parts.transpose(1, 0, 2).reshape(shard, -1).astype(f32)
+
+    return (
+        layer_out.astype(bf16).reshape(1, rows, width),
+        d_tokens.astype(bf16).reshape(1, rows, width),
+        t_attn,
+        columns(wq_g),
+        columns(wkv_g[:half]),
+        columns(wkv_g[half:]),
+        t_query,
+        t_key,
+        wo_g.reshape(ways * out_row, width).astype(f32),
+        t_post,
+        t_ffn,
+        hidden_whole(wg_g).astype(f32),
+        hidden_whole(wu_g).astype(f32),
+        wd_g.reshape(ways * hidden_row, width).astype(f32),
+        t_ffn_post,
+    )
+
+
 def solution(mesh):
     return jax.shard_map(
-        body,
+        plain_body if mesh.shape['ctx'] != HQ or mesh.shape['fsdp'] != 2 * HQ else split_body,
         mesh=mesh,
         in_specs=(
             P("fsdp", "ctx", None),

time: 1070 us -> 258 us (0.24)
  waiting for transfers between devices: 777 us -> 0 us
  Pallas kernels: 0 us -> 185 us
  blocking collectives: 175 us -> 0 us
  starting transfers between devices: 22.4 us -> 0 us
  matrix products: 36.2 us -> 18.7 us
  between operations: 18 us -> 1.8 us
  other arithmetic: 8.12 us -> 19.8 us
    reduce_scatter x10 -> x0, waiting for transfers between devices: 607 us -> none  [the longest x1 106 us: body(): lax.psum_scatter(grad_w_gate, 'fsdp', scatter_dimension=0, tiled=True)]
    pallas_call x0 -> x14, Pallas kernels: none -> 185 us  [the longest x7 99 us: gather(): pl.pallas_call(functools.partial(gather_kernel, axis, n, count), out_shap...]
    all_gather x5 -> x0, waiting for transfers between devices: 133 us -> none  [the longest x1 52 us: body(): lax.all_gather(w_up, 'fsdp', axis=0, tiled=True)]
    all_gather x9 -> x0, blocking collectives: 109 us -> none  [the longest x1 31.5 us: body(): lax.all_gather(w_value, 'fsdp', axis=0, tiled=True)]
    unnamed x2 -> x0, blocking collectives: 59.7 us -> none
    unnamed x23 -> x0, waiting for transfers between devices: 30.1 us -> none
    ppermute x16 -> x0, starting transfers between devices: 21.4 us -> none  [shifted_2(): lax.ppermute(value, axis, [(source, source + steps) for source in range(l...]
    dot_general x27 -> x23, matrix products: 36.2 us -> 18.7 us  [mul(): lax.dot_general(left, right, (dims, ((), ())), preferred_element_type=f32)]
  transfers between devices with their start and end apart: 35 -> 0, of which waited for: 20 -> 0; matrix products, arithmetic and copies ran while one was open for 5% -> 0% of each run, Pallas kernels for 0% -> 0%
where the time goes in v1:
time: 258 us; the launch traced here: 257 us
  Pallas kernels  185 us (72%)
  local copies, waits for them, and re-layouts  31.5 us (12%)
  other arithmetic  19.8 us (8%)
  matrix products  18.7 us (7%)
    pallas_call x7, Pallas kernels, gather(): pl.pallas_call(functools.partial(gather_kernel, axis, n, count), out_shap...  99 us
    pallas_call x5, Pallas kernels, add_scatter(): pl.pallas_call(functools.partial(add_scatter_kernel, axis, n, count), out...  75.2 us
    dot_general x23, matrix products, mul(): lax.dot_general(left, right, (dims, ((), ())), preferred_element_type=f32)  18.7 us
    unnamed x129, local copies, waits for them, and re-layouts  14 us
    pallas_call x2, Pallas kernels, swap(): pl.pallas_call(functools.partial(swap_kernel, axis, n), out_shape=jax.Sha...  10.7 us

profile of v1, /device:TPU:0, one launch (start us, length us, event | category | flops | bytes accessed | tf_op | source)
XLA Modules:
  0.0 256.7 jit_solution(2825243453533331602)
XLA Ops:
  0.7 4.2 %concatenate.37 = bf16[384]{0:T(512)(128)(2,1)S(1)} concatenate(bf16[80]{0:T(256)(128)(2,1)} %param.19, bf16[80]{0:T(256)(128)(2,1)} %param.26, bf16[80]{0:T(256)(128)(2,1)} %param.27, bf16[80]{0:T(256)(128)(2,1)} %param.31, bf16[32]{0:T(256)(128)(2,1)} %param.23, bf16[32]{0:T(256)(128)(2,1)} %param.24), dimensions={0} | concatenate | bytes 1536 | tf_op jit(solution)/shard_map/concatenate | solution.py:586
  7.2 1.2 copy.38
  9.1 51.6 %shard_map.271 = (bf16[8,96,768]{2,1,0:T(8,128)(2,1)S(1)}, bf16[8,32,640]{2,1,0:T(8,128)(2,1)S(1)}, bf16[8,80,512]{2,1,0:T(8,128)(2,1)S(1)}, bf16[8,80,512]{2,1,0:T(8,128)(2,1)S(1)}, bf16[8,64,640]{2,1,0:T(8,128)(2,1)S(1)}) custom-call(bf16[96,768]{1,0:T(8,128)(2,1)S(1)} %fusion.59.refs_0_, bf16[32,640]{1,0:T(8,128)(2,1)S(1)} %constant_dynamic-slice_fusion.3.refs_1_, ...), custom_call_target="tpu_custom_call" | custom-call | tf_op jit(solution)/shard_map/pallas_call | solution.py:388
  64.4 7.5 %shard_map.272 = (bf16[4,128,640]{2,1,0:T(8,128)(2,1)S(1)}, s32[4,8,128]{2,1,0:T(8,128)S(1)}) custom-call(bf16[128,640]{1,0:T(8,128)(2,1)S(1)} %fusion.33.refs_0_, s32[8,128]{1,0:T(8,128)S(1)} %broadcast_in_dim.27.refs_1_), custom_call_target="tpu_custom_call" | custom-call | tf_op jit(solution)/shard_map/pallas_call | solution.py:388
  73.8 1.3 mul.544
  77.1 1.3 mul.559
  79.1 1.6 fusion.75
  80.8 1.4 fusion.46
  84.0 5.4 %shard_map.273 = bf16[4,64,640]{2,1,0:T(8,128)(2,1)S(1)} custom-call(bf16[4,64,640]{2,1,0:T(8,128)(2,1)S(1)} %bitcast.146), custom_call_target="tpu_custom_call" | custom-call | tf_op jit(solution)/shard_map/pallas_call | solution.py:513
  89.8 7.9 %shard_map.274 = f32[128,640]{1,0:T(8,128)S(1)} custom-call(bf16[4,128,640]{2,1,0:T(8,128)(2,1)S(1)} %bitcast.128), custom_call_target="tpu_custom_call" | custom-call | tf_op jit(solution)/shard_map/pallas_call | solution.py:469
  98.3 7.1 %shard_map.275 = bf16[4,128,640]{2,1,0:T(8,128)(2,1)S(1)} custom-call(bf16[128,640]{1,0:T(8,128)(2,1)S(1)} %multiply_convert_fusion.3.refs_0_), custom_call_target="tpu_custom_call" | custom-call | tf_op jit(solution)/shard_map/pallas_call | solution.py:388
  106.5 1.6 multiply_convert_fusion.2
  108.7 8.0 %shard_map.276 = f32[128,640]{1,0:T(8,128)S(1)} custom-call(bf16[4,128,640]{2,1,0:T(8,128)(2,1)S(1)} %bitcast.140), custom_call_target="tpu_custom_call" | custom-call | tf_op jit(solution)/shard_map/pallas_call | solution.py:469
  116.9 1.2 fusion.40
  118.1 1.8 fusion.36
  119.9 7.0 %shard_map.277 = bf16[4,128,640]{2,1,0:T(8,128)(2,1)S(1)} custom-call(bf16[128,640]{1,0:T(8,128)(2,1)S(1)} %get-tuple-element.102.refs_0_), custom_call_target="tpu_custom_call" | custom-call | tf_op jit(solution)/shard_map/pallas_call | solution.py:388
  126.9 2.7 %multiply_convert_fusion.1 = (bf16[512,512]{1,0:T(8,128)(2,1)S(1)}, bf16[512,512]{1,0:T(8,128)(2,1)S(1)}) fusion(f32[512,512]{1,0:T(8,128)S(1)} %copy-done.25, f32[512,512]{1,0:T(8,128)} %get-tuple-element.127, bf16[512,640]{1,0:T(8,128)(2,1)S(1)} %bitcast.138, bf16[512,640]{1,0:T(8,128)(2,1)S(1)} %bitcast.149), kind=kOutput, calls=%fused_computation.35 | convolution fusion | flops 341835776 | bytes 4456448 | tf_op jit(solution)/shard_map/dot_general | solution.py:562
  131.8 8.0 %shard_map.278 = f32[128,640]{1,0:T(8,128)S(1)} custom-call(bf16[4,128,640]{2,1,0:T(8,128)(2,1)S(1)} %bitcast.132), custom_call_target="tpu_custom_call" | custom-call | tf_op jit(solution)/shard_map/pallas_call | solution.py:469
  140.4 7.1 %shard_map.279 = bf16[4,128,640]{2,1,0:T(8,128)(2,1)S(1)} custom-call(bf16[128,640]{1,0:T(8,128)(2,1)S(1)} %fusion.37.refs_0_), custom_call_target="tpu_custom_call" | custom-call | tf_op jit(solution)/shard_map/pallas_call | solution.py:388
  151.3 1.9 multiply_cosine_fusion
  153.7 1.5 convolution_convert_fusion
  155.3 11.0 %shard_map.280 = f32[128,1152]{1,0:T(8,128)S(1)} custom-call(bf16[4,128,1152]{2,1,0:T(8,128)(2,1)S(1)} %pad_maximum_fusion.refs_0_), custom_call_target="tpu_custom_call" | custom-call | tf_op jit(solution)/shard_map/pallas_call | solution.py:469
  170.5 1.6 fusion.34
  172.9 1.4 convolution_convert_fusion.4
  174.3 1.4 convolution_convert_fusion.3
  175.6 1.4 convolution_convert_fusion.2
  177.9 5.3 %shard_map.281 = bf16[4,64,640]{2,1,0:T(8,128)(2,1)S(1)} custom-call(bf16[4,64,640]{2,1,0:T(8,128)(2,1)S(1)} %bitcast.134), custom_call_target="tpu_custom_call" | custom-call | tf_op jit(solution)/shard_map/pallas_call | solution.py:513
  183.3 7.3 %shard_map.282 = bf16[4,128,512]{2,1,0:T(8,128)(2,1)S(1)} custom-call(bf16[128,512]{1,0:T(8,128)(2,1)S(1)} %pad_maximum_fusion.7.refs_0_), custom_call_target="tpu_custom_call" | custom-call | tf_op jit(solution)/shard_map/pallas_call | solution.py:388
  193.9 40.4 %shard_map.283 = (bf16[80,512]{1,0:T(8,128)(2,1)S(1)}, bf16[80,512]{1,0:T(8,128)(2,1)S(1)}, bf16[64,640]{1,0:T(8,128)(2,1)S(1)}, bf16[80,256]{1,0:T(8,128)(2,1)S...) custom-call(bf16[8,80,512]{2,1,0:T(8,128)(2,1)S(1)} %bitcast.143, ...), custom_call_target="tpu_custom_call" | custom-call | tf_op jit(solution)/shard_map/pallas_call | solution.py:469
  234.3 11.4 %shard_map.284 = (bf16[4,80,512]{2,1,0:T(8,128)(2,1)S(1)}, bf16[4,80,512]{2,1,0:T(8,128)(2,1)S(1)}, bf16[4,64,640]{2,1,0:T(8,128)(2,1)S(1)}, bf16[4,80,256]{2,1,...) custom-call(bf16[80,512]{1,0:T(8,128)(2,1)S(1)} %get-tuple-element.4, ...), custom_call_target="tpu_custom_call" | custom-call | tf_op jit(solution)/shard_map/pallas_call | solution.py:388
  250.0 1.5 copy.46
  251.5 2.4 copy.48
  (223 shorter events, 38.6 us)
Async XLA Ops:
  0.6 8.4 %copy-start = (bf16[256,640]{1,0:T(8,128)(2,1)S(1)}, bf16[256,640]{1,0:T(8,128)(2,1)}, u32[]{:S(2)}) copy-start(bf16[256,640]{1,0:T(8,128)(2,1)} %param.30) | copy-start | bytes 983044
  0.7 7.8 %copy-start.32 = (bf16[80,2048]{1,0:T(8,128)(2,1)S(1)}, bf16[80,2048]{1,0:T(8,128)(2,1)}, u32[]{:S(2)}) copy-start(bf16[80,2048]{1,0:T(8,128)(2,1)} %param.28) | copy-start | bytes 983044
  8.5 55.3 %copy-start.19 = (bf16[1,128,640]{2,1,0:T(8,128)(2,1)S(1)}, bf16[1,128,640]{2,1,0:T(8,128)(2,1)}, u32[]{:S(2)}) copy-start(bf16[1,128,640]{2,1,0:T(8,128)(2,1)} %param.16) | copy-start | bytes 491524
  8.5 55.9 %copy-start.59 = (s32[1,128]{1,0:T(1,128)S(1)}, s32[1,128]{1,0:T(1,128)}, u32[]{:S(2)}) copy-start(s32[1,128]{1,0:T(1,128)} %param.17) | copy-start | bytes 1540
  73.0 10.2 %copy-start.12 = (f32[512,768]{1,0:T(8,128)}, f32[512,768]{1,0:T(8,128)S(1)}, u32[]{:S(2)}) copy-start(f32[512,768]{1,0:T(8,128)S(1)} %fusion.81) | copy-start | bytes 4718596
  80.7 1.9 copy-start.55
  84.0 13.8 %copy-start.22 = (bf16[512,256]{1,0:T(8,128)(2,1)}, bf16[512,256]{1,0:T(8,128)(2,1)S(1)}, u32[]{:S(2)}) copy-start(bf16[512,256]{1,0:T(8,128)(2,1)S(1)} %convolution_convert_fusion.9) | copy-start | bytes 786436
  89.4 8.7 %copy-start.17 = (bf16[4,2,32,640]{3,2,0,1:T(8,128)(2,1)}, bf16[4,2,32,640]{3,2,0,1:T(8,128)(2,1)S(1)}, u32[]{:S(2)}) copy-start(bf16[4,2,32,640]{3,2,0,1:T(8,128)(2,1)S(1)} %copy.40) | copy-start | bytes 983044
  89.4 8.5 %copy-start.20 = (bf16[1,128,640]{2,1,0:T(8,128)(2,1)S(1)}, bf16[1,128,640]{2,1,0:T(8,128)(2,1)}, u32[]{:S(2)}) copy-start(bf16[1,128,640]{2,1,0:T(8,128)(2,1)} %param.16) | copy-start | bytes 491524
  89.4 8.5 %copy-start.43 = (f32[640]{0:T(1024)S(1)}, f32[640]{0:T(1024)}, u32[]{:S(2)}) copy-start(f32[640]{0:T(1024)} %mul.571) | copy-start | bytes 7684
  89.8 8.3 %copy-start.51 = (f32[8,80]{1,0:T(8,128)S(1)}, f32[8,80]{1,0:T(8,128)}, u32[]{:S(2)}) copy-start(f32[8,80]{1,0:T(8,128)} %get-tuple-element.107) | copy-start | bytes 7684
  106.0 2.1 copy-start.24
  108.1 8.6 %copy-start.60 = (bf16[512,512]{1,0:T(8,128)(2,1)}, bf16[512,512]{1,0:T(8,128)(2,1)S(1)}, u32[]{:S(2)}) copy-start(bf16[512,512]{1,0:T(8,128)(2,1)S(1)} %get-tuple-element.126) | copy-start | bytes 1572868
  108.1 8.7 %copy-start.50 = (f32[8,80]{1,0:T(8,128)S(1)}, f32[8,80]{1,0:T(8,128)}, u32[]{:S(2)}) copy-start(f32[8,80]{1,0:T(8,128)} %get-tuple-element.106) | copy-start | bytes 7684
  116.9 10.0 %copy-start.11 = (bf16[8,64,640]{2,1,0:T(8,128)(2,1)S(1)}, bf16[8,64,640]{2,1,0:T(8,128)(2,1)}, u32[]{:S(2)}) copy-start(bf16[8,64,640]{2,1,0:T(8,128)(2,1)} %copy-done.9) | copy-start | bytes 1966084
  116.9 10.0 %copy-start.25 = (f32[512,512]{1,0:T(8,128)S(1)}, f32[512,512]{1,0:T(8,128)}, u32[]{:S(2)}) copy-start(f32[512,512]{1,0:T(8,128)} %copy-done.24) | copy-start | bytes 3145732
  126.9 2.7 %copy-start.1 = (bf16[4,128,640]{2,1,0:T(8,128)(2,1)}, bf16[4,128,640]{2,1,0:T(8,128)(2,1)S(1)}, u32[]{:S(2)}) copy-start(bf16[4,128,640]{2,1,0:T(8,128)(2,1)S(1)} %shard_map.277) | copy-start | bytes 1966084
  129.6 2.1 copy-start.28
  129.7 2.1 copy-start.30
  131.8 8.1 %copy-start.21 = (bf16[1,128,640]{2,1,0:T(8,128)(2,1)S(1)}, bf16[1,128,640]{2,1,0:T(8,128)(2,1)}, u32[]{:S(2)}) copy-start(bf16[1,128,640]{2,1,0:T(8,128)(2,1)} %param.18) | copy-start | bytes 491524
  139.9 7.5 %copy-start.18 = (bf16[4,2,32,640]{3,2,0,1:T(8,128)(2,1)S(1)}, bf16[4,2,32,640]{3,2,0,1:T(8,128)(2,1)}, u32[]{:S(2)}) copy-start(bf16[4,2,32,640]{3,2,0,1:T(8,128)(2,1)} %copy-done.17) | copy-start | bytes 983044
  140.2 7.6 %copy-start.16 = (f32[512,512]{0,1:T(8,128)S(1)}, f32[512,512]{0,1:T(8,128)}, u32[]{:S(2)}) copy-start(f32[512,512]{0,1:T(8,128)} %copy-done.15) | copy-start | bytes 3145732
  150.9 2.3 copy-start.46
  150.9 2.3 copy-start.52
  151.3 2.2 copy-start.48
  155.3 13.0 %copy-start.49 = (f32[256]{0:T(256)S(1)}, f32[256]{0:T(256)}, u32[]{:S(2)}) copy-start(f32[256]{0:T(256)} %mul.559) | copy-start | bytes 3076
  155.3 15.1 %copy-start.45 = (f32[640]{0:T(1024)S(1)}, f32[640]{0:T(1024)}, u32[]{:S(2)}) copy-start(f32[640]{0:T(1024)} %copy-done.44) | copy-start | bytes 7684
  155.3 15.1 %copy-start.54 = (f32[128]{0:T(128)S(1)}, f32[128]{0:T(128)}, u32[]{:S(2)}) copy-start(f32[128]{0:T(128)} %copy-done.53) | copy-start | bytes 1540
  167.3 4.8 %copy-start.58 = (f32[128]{0:T(128)S(1)}, f32[128]{0:T(128)}, u32[]{:S(2)}) copy-start(f32[128]{0:T(128)} %copy-done.57) | copy-start | bytes 1540
  170.4 2.5 copy-start.29
  172.1 2.2 copy-start.31
  177.9 13.8 %copy-start.6 = (bf16[640,512]{1,0:T(8,128)(2,1)S(1)}, bf16[640,512]{1,0:T(8,128)(2,1)}, u32[]{:S(2)}) copy-start(bf16[640,512]{1,0:T(8,128)(2,1)} %convolution_convert_fusion.4) | copy-start | bytes 1966084
  (30 other events, 31.7 us)

commit v2 on v1

--- a/solution.py
+++ b/solution.py
@@ -337,9 +337,10 @@
     pl.semaphore_wait(barrier, len(indices))
 
 
-def gather_kernel(axis, n, count, *refs):
-    ins, outs = refs[:count], refs[count : 2 * count]
-    send, recv = refs[2 * count :]
+def gather_kernel(axis, n, count, swaps, *refs):
+    every = count + swaps
+    ins, outs = refs[:every], refs[every : 2 * every]
+    send, recv = refs[2 * every :]
     me = lax.axis_index(axis)
     outer, inner = lax.div(me, 2), lax.rem(me, 2)
     span = n // 2
@@ -351,7 +352,20 @@
     def behind(step):
         return lax.rem(outer + span - step, span)
 
-    greet(axis, [twin] + [ahead(step) for step in range(1, span)])
+    if swaps:
+        greet(axis, [lax.rem(me + step, n) for step in range(1, n)])
+    else:
+        greet(axis, [twin] + [ahead(step) for step in range(1, span)])
+
+    def trade(i, step, slot):
+        target = lax.rem(me + step, n)
+        return pltpu.make_async_remote_copy(
+            src_ref=ins[i].at[target],
+            dst_ref=outs[i].at[slot],
+            send_sem=send.at[i, step - 1],
+            recv_sem=recv.at[i, step - 1],
+            **peer_of(axis, target),
+        )
 
     def copy(i, source, slot, lane, target):
         return pltpu.make_async_remote_copy(
@@ -366,8 +380,13 @@
         for step in range(1, span):
             copy(i, ins[i], me, step, ahead(step)).start()
         copy(i, ins[i], me, 0, twin).start()
+    for i in range(count, every):
+        for step in range(1, n):
+            trade(i, step, me).start()
     for i in range(count):
         outs[i][me] = ins[i][...]
+    for i in range(count, every):
+        outs[i][me] = ins[i][me]
     for i in range(count):
         for step in range(1, span):
             slot = behind(step) * 2 + inner
@@ -380,14 +399,22 @@
             copy(i, ins[i], slot, span - 1 + step, twin).wait_recv()
         for lane in range(2 * span - 1):
             copy(i, ins[i], me, lane, twin).wait_send()
-
-
-def gather(axis, n, key, *arrays):
+    for i in range(count, every):
+        for step in range(1, n):
+            trade(i, step, lax.rem(me + n - step, n)).wait_recv()
+        for step in range(1, n):
+            trade(i, step, me).wait_send()
+
+
+def gather(axis, n, key, *arrays, swapped=()):
+    kept = len(arrays)
+    shapes = [(n,) + a.shape for a in arrays] + [a.shape for a in swapped]
+    arrays = arrays + swapped
     count = len(arrays)
     spec = pl.BlockSpec(memory_space=pltpu.VMEM)
     return pl.pallas_call(
-        functools.partial(gather_kernel, axis, n, count),
-        out_shape=[jax.ShapeDtypeStruct((n,) + a.shape, a.dtype) for a in arrays],
+        functools.partial(gather_kernel, axis, n, kept, len(swapped)),
+        out_shape=[jax.ShapeDtypeStruct(shape, a.dtype) for shape, a in zip(shapes, arrays)],
         in_specs=[spec] * count,
         out_specs=[spec] * count,
         scratch_shapes=[
@@ -482,44 +509,129 @@
     )(*arrays)
 
 
-def swap_kernel(axis, n, in_ref, out_ref, send, recv):
-    me = lax.axis_index(axis)
+def finish_kernel(owners, ways, sums, count, *refs):
+    ins, outs = refs[:count], refs[count : 2 * count]
+    refs = refs[2 * count :]
+    from_twin, paired, landed = refs[:sums], refs[sums : 2 * sums], refs[2 * sums : 3 * sums]
+    send, recv, send_ctx, recv_ctx = refs[3 * sums :]
+    f32 = jnp.float32
+    me = lax.axis_index("fsdp")
+    outer, inner = lax.div(me, 2), lax.rem(me, 2)
+    span = owners // 2
+    twin = outer * 2 + (1 - inner)
+    part = lax.axis_index("ctx")
+    side, core = lax.div(part, 2), lax.rem(part, 2)
+    reach = ways // 2
+    mate = side * 2 + (1 - core)
 
     def ahead(step):
-        return lax.rem(me + step, n)
-
-    greet(axis, [ahead(step) for step in range(1, n)])
-
-    def copy(step, slot):
+        return lax.rem(outer + step, span)
+
+    def across(step):
+        return lax.rem(side + step, reach) * 2 + core
+
+    def behind(step):
+        return lax.rem(side + reach - step, reach)
+
+    barrier = pltpu.get_barrier_semaphore()
+    fsdp_peers = [twin] + [ahead(step) * 2 + inner for step in range(1, span)]
+    ctx_peers = [mate] + [across(step) for step in range(1, reach)]
+    for index in fsdp_peers:
+        pl.semaphore_signal(barrier, inc=1, **peer_of("fsdp", index))
+    for index in ctx_peers:
+        pl.semaphore_signal(barrier, inc=1, **peer_of("ctx", index))
+    pl.semaphore_wait(barrier, len(fsdp_peers) + len(ctx_peers))
+
+    def to_twin(i, step):
         return pltpu.make_async_remote_copy(
-            src_ref=in_ref.at[ahead(step)],
-            dst_ref=out_ref.at[slot],
-            send_sem=send.at[step],
-            recv_sem=recv.at[step],
-            **peer_of(axis, ahead(step)),
+            src_ref=ins[i].at[ahead(step) * 2 + (1 - inner)],
+            dst_ref=from_twin[i].at[step],
+            send_sem=send.at[i, step],
+            recv_sem=recv.at[i, step],
+            **peer_of("fsdp", twin),
         )
 
-    for step in range(1, n):
-        copy(step, me).start()
-    out_ref[me] = in_ref[me]
-    for step in range(1, n):
-        copy(step, lax.rem(me + n - step, n)).wait_recv()
-    for step in range(1, n):
-        copy(step, me).wait_send()
-
-
-def swap(axis, n, key, array):
+    def to_owner(i, step):
+        return pltpu.make_async_remote_copy(
+            src_ref=paired[i].at[step],
+            dst_ref=landed[i].at[step],
+            send_sem=send.at[i, span + step],
+            recv_sem=recv.at[i, span + step],
+            **peer_of("fsdp", ahead(step) * 2 + inner),
+        )
+
+    def spread(i, slot, lane, target):
+        return pltpu.make_async_remote_copy(
+            src_ref=outs[i].at[slot],
+            dst_ref=outs[i].at[slot],
+            send_sem=send_ctx.at[i, lane],
+            recv_sem=recv_ctx.at[i, lane],
+            **peer_of("ctx", target),
+        )
+
+    def publish(i):
+        for step in range(1, reach):
+            spread(i, part, step, across(step)).start()
+        spread(i, part, 0, mate).start()
+
+    for i in range(sums):
+        for step in list(range(1, span)) + [0]:
+            to_twin(i, step).start()
+    for i in range(sums, count):
+        outs[i][part] = ins[i][...]
+        publish(i)
+    for i in range(sums):
+        for step in range(1, span):
+            to_twin(i, step).wait_recv()
+            paired[i][step] = (
+                ins[i][ahead(step) * 2 + inner].astype(f32) + from_twin[i][step].astype(f32)
+            ).astype(paired[i].dtype)
+            to_owner(i, step).start()
+    for i in range(sums):
+        to_twin(i, 0).wait_recv()
+        total = ins[i][me].astype(f32) + from_twin[i][0].astype(f32)
+        for step in range(1, span):
+            to_owner(i, step).wait_recv()
+            total = total + landed[i][step].astype(f32)
+        outs[i][part] = total.astype(outs[i].dtype)
+        publish(i)
+    turn = list(range(sums, count)) + list(range(sums))
+    for i in turn:
+        for step in range(1, reach):
+            slot = behind(step) * 2 + core
+            spread(i, slot, step, mate).wait_recv()
+            spread(i, slot, reach - 1 + step, mate).start()
+    for i in turn:
+        spread(i, mate, 0, mate).wait_recv()
+        for step in range(1, reach):
+            spread(i, behind(step) * 2 + (1 - core), reach - 1 + step, mate).wait_recv()
+        for lane in range(2 * reach - 1):
+            spread(i, part, lane, mate).wait_send()
+    for i in range(sums):
+        for step in range(span):
+            to_twin(i, step).wait_send()
+        for step in range(1, span):
+            to_owner(i, step).wait_send()
+
+
+def finish(owners, ways, key, summed, others):
+    arrays = summed + others
+    sums, count = len(summed), len(arrays)
     spec = pl.BlockSpec(memory_space=pltpu.VMEM)
+    shapes = [(ways,) + a.shape[1:] for a in summed] + [(ways,) + a.shape for a in others]
+    slots = [pltpu.VMEM((owners // 2,) + a.shape[1:], a.dtype) for a in summed]
     return pl.pallas_call(
-        functools.partial(swap_kernel, axis, n),
-        out_shape=jax.ShapeDtypeStruct(array.shape, array.dtype),
-        in_specs=[spec],
-        out_specs=spec,
-        scratch_shapes=[pltpu.SemaphoreType.DMA((n,)), pltpu.SemaphoreType.DMA((n,))],
+        functools.partial(finish_kernel, owners, ways, sums, count),
+        out_shape=[jax.ShapeDtypeStruct(shape, a.dtype) for shape, a in zip(shapes, arrays)],
+        in_specs=[spec] * count,
+        out_specs=[spec] * count,
+        scratch_shapes=slots * 3
+        + [pltpu.SemaphoreType.DMA((sums, owners))] * 2
+        + [pltpu.SemaphoreType.DMA((count, ways - 1))] * 2,
         compiler_params=pltpu.CompilerParams(
             collective_id=key, has_side_effects=True, vmem_limit_bytes=VMEM_BYTES
         ),
-    )(array)
+    )(*arrays)
 
 
 def turned_norm(values, gain_vec, cosine, sine_table):
@@ -596,15 +708,25 @@
         ],
         axis=0,
     )
-    attn_all, wo_rows, wg_all, wu_all, wd_all = gather(
+    hidden_cols = owners * hidden_row
+    wgu_part = lax.all_gather(
+        jnp.concatenate([hidden_part(w_gate), hidden_part(w_up)], axis=1),
+        "fsdp",
+        axis=0,
+        tiled=True,
+    )
+    wd_part = lax.all_gather(
+        lax.dynamic_slice_in_dim(w_down, part * hidden_row, hidden_row, 0),
+        "fsdp",
+        axis=0,
+        tiled=True,
+    )
+    attn_all, wo_rows = gather(
         "fsdp",
         owners,
         0,
         attn_pack,
         lax.dynamic_slice_in_dim(w_output, part * out_row, out_row, 0),
-        hidden_part(w_gate),
-        hidden_part(w_up),
-        lax.dynamic_slice_in_dim(w_down, part * hidden_row, hidden_row, 0),
     )
     gains = attn_all[:, shard, :gain_size].astype(f32)
 
@@ -616,19 +738,19 @@
     g_key = gains[:, 4 * shard + head_share :].reshape(HD)
     w_qkv = attn_all[:, :shard].reshape(width, 3 * HD)
     wq_head, wk_full, wv_full = (w_qkv[:, i * HD : (i + 1) * HD] for i in range(3))
-    wg_part = wg_all.reshape(width, owners * hidden_row)
-    wu_part = wu_all.reshape(width, owners * hidden_row)
-    wd_part = wd_all.reshape(owners * hidden_row, width)
+    attn_in = rms_gain(inputs, g_attn).astype(bf16)
+    attn_seq, place_all, wo_head = gather(
+        "ctx",
+        ways,
+        2,
+        attn_in,
+        jnp.broadcast_to(positions.reshape(1, rows), (8, rows)),
+        swapped=(wo_rows.reshape(ways, owners // ways * out_row, width),),
+    )
     wo_head = (
-        swap("ctx", ways, 1, wo_rows.reshape(ways, owners // ways * out_row, width))
-        .reshape(ways, owners // ways, out_row, width)
+        wo_head.reshape(ways, owners // ways, out_row, width)
         .transpose(1, 0, 2, 3)
         .reshape(HD, width)
-    )
-
-    attn_in = rms_gain(inputs, g_attn).astype(bf16)
-    attn_seq, place_all = gather(
-        "ctx", ways, 2, attn_in, jnp.broadcast_to(positions.reshape(1, rows), (8, rows))
     )
     attn_seq = attn_seq.reshape(seq, width)
     seq_place = place_all[:, 0].reshape(seq)
@@ -662,8 +784,8 @@
     branch = own_sum(3, nn(att_low, wo_head))
     hidden_res = inputs + rms_gain(branch, g_post)
     ffn_seq = whole(4, rms_gain(hidden_res, g_ffn).astype(bf16))
-    gate_proj = nn(ffn_seq, wg_part)
-    up_proj = nn(ffn_seq, wu_part)
+    gate_up = nn(ffn_seq, wgu_part)
+    gate_proj, up_proj = gate_up[:, :hidden_cols], gate_up[:, hidden_cols:]
     mixed_low = gated_gelu(gate_proj, up_proj).astype(bf16)
     down_out = own_sum(5, nn(mixed_low, wd_part))
     layer_out = hidden_res + rms_gain(down_out, g_ffn_post)
@@ -672,12 +794,14 @@
     d_down_seq = whole(6, d_down.astype(bf16))
     d_mixed = nt(d_down_seq, wd_part)
     d_gate, d_up = jax.vjp(gated_gelu, gate_proj, up_proj)[1](d_mixed)
-    d_gate_low = d_gate.astype(bf16)
-    d_up_low = d_up.astype(bf16)
-    d_ffn_in = own_sum(7, nt(d_gate_low, wg_part) + nt(d_up_low, wu_part))
-    grad_w_down = tn(mixed_low, d_down_seq)
-    grad_w_gate = tn(ffn_seq, d_gate_low)
-    grad_w_up = tn(ffn_seq, d_up_low)
+    d_gate_up = jnp.concatenate([d_gate.astype(bf16), d_up.astype(bf16)], axis=1)
+    d_ffn_in = own_sum(7, nt(d_gate_up, wgu_part))
+    wd_g = lax.psum_scatter(
+        tn(mixed_low, d_down_seq).astype(bf16), "fsdp", scatter_dimension=0, tiled=True
+    )
+    wgu_g = lax.psum_scatter(
+        tn(ffn_seq, d_gate_up).astype(bf16), "fsdp", scatter_dimension=0, tiled=True
+    )
     d_hidden_part, d_ffn_norm = jax.vjp(rms_gain, hidden_res, g_ffn)[1](d_ffn_in)
     d_hidden = grad_out + d_hidden_part
 
@@ -704,22 +828,26 @@
     )[1](sums[:, width : width + HD])
     dkv_low = jnp.concatenate([d_k_pre, sums[:, width + HD :]], axis=1).astype(bf16)
     d_attn_in = sums[:, :width] + nt(dkv_low, w_qkv[:, HD:])
-    dkv_seq = whole(10, dkv_low)
+    dkv_seq, grad_wo_rows = gather(
+        "ctx",
+        ways,
+        10,
+        dkv_low,
+        swapped=(
+            grad_w_output.astype(bf16)
+            .reshape(owners // ways, ways, out_row, width)
+            .transpose(1, 0, 2, 3)
+            .reshape(ways, owners // ways * out_row, width),
+        ),
+    )
+    dkv_seq = dkv_seq.reshape(seq, 2 * HD)
+    grad_wo_rows = grad_wo_rows.reshape(owners, out_row, width)
     d_inputs_part, d_attn_norm = jax.vjp(rms_gain, inputs, g_attn)[1](d_attn_in)
     d_tokens = d_hidden + d_inputs_part
     grad_w_query = tn(attn_seq, dq_low)
     dkv_cols = 2 * HD // ways
     grad_w_kv = tn(attn_seq, lax.dynamic_slice_in_dim(dkv_seq, part * dkv_cols, dkv_cols, 1))
 
-    grad_wo_rows = swap(
-        "ctx",
-        ways,
-        11,
-        grad_w_output.astype(bf16)
-        .reshape(owners // ways, ways, out_row, width)
-        .transpose(1, 0, 2, 3)
-        .reshape(ways, owners // ways * out_row, width),
-    ).reshape(owners, out_row, width)
     gain_grads = jnp.concatenate(
         [
             value.reshape(owners, -1)
@@ -732,20 +860,13 @@
     def blocks(value):
         return value.astype(bf16).reshape(owners, value.shape[0] // owners, value.shape[1])
 
-    mine = add_scatter(
-        "fsdp",
+    wq_g, wo_g, wkv_g, gain_g, wgu_g, wd_g = finish(
         owners,
+        ways,
         12,
-        bf16,
-        blocks(grad_w_gate),
-        blocks(grad_w_up),
-        blocks(grad_w_down),
-        blocks(grad_w_query),
-        grad_wo_rows,
-        blocks(grad_w_kv),
-        gain_grads.astype(bf16),
-    )
-    wg_g, wu_g, wd_g, wq_g, wo_g, wkv_g, gain_g = gather("ctx", ways, 13, *mine)
+        [blocks(grad_w_query), grad_wo_rows, blocks(grad_w_kv), gain_grads.astype(bf16)],
+        [wgu_g, wd_g],
+    )
     gain_sum = jnp.sum(gain_g[:, 0].astype(f32), axis=0)
     ends = [shard * i for i in range(1, 5)] + [4 * shard + head_share]
     t_attn, t_post, t_ffn, t_ffn_post, t_query, t_key = jnp.split(gain_sum, ends)
@@ -766,8 +887,8 @@
         wo_g.reshape(ways * out_row, width).astype(f32),
         t_post,
         t_ffn,
-        hidden_whole(wg_g).astype(f32),
-        hidden_whole(wu_g).astype(f32),
+        hidden_whole(wgu_g[:, :, :hidden_cols]).astype(f32),
+        hidden_whole(wgu_g[:, :, hidden_cols:]).astype(f32),
         wd_g.reshape(ways * hidden_row, width).astype(f32),
         t_ffn_post,
     )

time: 258 us -> 311 us (1.21)
  waiting for transfers between devices: 0 us -> 72.6 us
  Pallas kernels: 185 us -> 125 us
  blocking collectives: 0 us -> 36.6 us
  between operations: 1.8 us -> 14.7 us
  local copies, waits for them, and re-layouts: 31.5 us -> 20.7 us
  matrix products: 18.7 us -> 23.7 us
  other arithmetic: 19.8 us -> 15.6 us
    reduce_scatter x0 -> x2, waiting for transfers between devices: none -> 72.6 us  [the longest x1 67.1 us: split_body(): lax.psum_scatter(tn(ffn_seq, d_gate_up).astype(bf16), 'fsdp', scatter_dim...]
    pallas_call x5 -> x4, Pallas kernels: 75.2 us -> 34.6 us  [add_scatter(): pl.pallas_call(functools.partial(add_scatter_kernel, axis, n, count), out...]
    all_gather x0 -> x1, blocking collectives: none -> 36.6 us  [split_body(): lax.all_gather(lax.dynamic_slice_in_dim(w_down, part * hidden_row, hidden...]
    pallas_call x9 -> x7, Pallas kernels: 110 us -> 90.8 us  [the longest x6 69.9 us: gather(): pl.pallas_call(functools.partial(gather_kernel, axis, n, kept, len(swappe...]
    dot_general x23 -> x20, matrix products: 18.7 us -> 23.7 us  [mul(): lax.dot_general(left, right, (dims, ((), ())), preferred_element_type=f32)]
    concatenate x1, local copies, waits for them, and re-layouts: 4.16 us -> 0.1 us  [split_body(): jnp.concatenate([attn_norm, attn_post_norm, ffn_norm, ffn_post_norm, quer...]
    unnamed x129 -> x89, local copies, waits for them, and re-layouts: 14 us -> 10.7 us
  transfers between devices with their start and end apart: 0 -> 3, of which waited for: 0 -> 2; matrix products, arithmetic and copies ran while one was open for 0% -> 10% of each run, Pallas kernels for 0% -> 29%
where the time goes in v2:
time: 311 us; the launch traced here: 310 us
  Pallas kernels  125 us (40%)
  waiting for transfers between devices  72.6 us (23%)
  blocking collectives  36.6 us (12%)
  matrix products  23.7 us (8%)
  local copies, waits for them, and re-layouts  20.7 us (7%)
  other arithmetic  15.6 us (5%)
  between operations  14.7 us (5%)
    pallas_call x6, Pallas kernels, gather(): pl.pallas_call(functools.partial(gather_kernel, axis, n, kept, len(swappe...  69.9 us
    reduce_scatter x1, waiting for transfers between devices, split_body(): lax.psum_scatter(tn(ffn_seq, d_gate_up).astype(bf16), 'fsdp', scatter_dim...  67.1 us
    all_gather x1, blocking collectives, split_body(): lax.all_gather(lax.dynamic_slice_in_dim(w_down, part * hidden_row, hidden...  36.6 us
    pallas_call x4, Pallas kernels, add_scatter(): pl.pallas_call(functools.partial(add_scatter_kernel, axis, n, count), out...  34.6 us
    dot_general x20, matrix products, mul(): lax.dot_general(left, right, (dims, ((), ())), preferred_element_type=f32)  23.7 us
    pallas_call x1, Pallas kernels, finish(): pl.pallas_call(functools.partial(finish_kernel, owners, ways, sums, count...  20.9 us
    unnamed x89, local copies, waits for them, and re-layouts  10.7 us
  transfers between devices with their start and end apart: 3, of which 2 were waited for; matrix products, arithmetic and copies ran while one was open for 10% of the time, Pallas kernels for 29%

profile of v2, /device:TPU:0, one launch (start us, length us, event | category | flops | bytes accessed | tf_op | source)
XLA Modules:
  0.0 309.7 jit_solution(659501945367129239)
XLA Ops:
  7.3 1.3 copy.37
  8.7 1.2 copy.39
  12.7 30.7 %shard_map.271 = (bf16[8,96,768]{2,1,0:T(8,128)(2,1)S(1)}, bf16[8,32,640]{2,1,0:T(8,128)(2,1)S(1)}) custom-call(bf16[96,768]{1,0:T(8,128)(2,1)S(1)} %fusion.58.refs_0_, bf16[32,640]{1,0:T(8,128)(2,1)S(1)} %constant_dynamic-slice_fusion.3.refs_1_), custom_call_target="tpu_custom_call" | custom-call | tf_op jit(solution)/shard_map/pallas_call | solution.py:415
  45.0 9.7 %shard_map.272 = (bf16[4,128,640]{2,1,0:T(8,128)(2,1)S(1)}, s32[4,8,128]{2,1,0:T(8,128)S(1)}, bf16[4,64,640]{2,1,0:T(8,128)(2,1)S(1)}) custom-call(bf16[128,640]{1,0:T(8,128)(2,1)S(1)} %fusion.32.refs_0_, s32[8,128]{1,0:T(8,128)S(1)} %broadcast_in_dim.27.refs_1_, bf16[4,64,640]{2,1,0:T(8,128)(2,1)S(1)} %bitcast.121), custom_call_target="tpu_custom_call" | custom-call | tf_op jit(solution)/shard_map/pallas_call | solution.py:415
  54.7 2.0 fusion.82
  58.1 1.2 fusion.45
  61.5 8.3 %shard_map.273 = f32[128,640]{1,0:T(8,128)S(1)} custom-call(bf16[4,128,640]{2,1,0:T(8,128)(2,1)S(1)} %bitcast.108), custom_call_target="tpu_custom_call" | custom-call | tf_op jit(solution)/shard_map/pallas_call | solution.py:496
  70.5 6.9 %shard_map.274 = bf16[4,128,640]{2,1,0:T(8,128)(2,1)S(1)} custom-call(bf16[128,640]{1,0:T(8,128)(2,1)S(1)} %multiply_convert_fusion.3.refs_0_), custom_call_target="tpu_custom_call" | custom-call | tf_op jit(solution)/shard_map/pallas_call | solution.py:415
  78.6 36.6 %all_gather.7 = bf16[512,640]{1,0:T(8,128)(2,1)} all-gather(bf16[64,640]{1,0:T(8,128)(2,1)S(1)} %constant_dynamic-slice_fusion), channel_id=1, replica_groups=mesh['fsdp'=8,'ctx'=4] {'fsdp'}, dimensions={0}, use_global_device_ids=true | all-gather | bytes 737280 | tf_op jit(solution)/shard_map/all_gather | solution.py:718
  115.2 2.3 fusion.83
  117.9 1.2 copy-done.19
  119.7 7.3 %shard_map.275 = f32[128,640]{1,0:T(8,128)S(1)} custom-call(bf16[4,128,640]{2,1,0:T(8,128)(2,1)S(1)} %bitcast.119), custom_call_target="tpu_custom_call" | custom-call | tf_op jit(solution)/shard_map/pallas_call | solution.py:496
  128.1 7.3 %shard_map.276 = bf16[4,128,640]{2,1,0:T(8,128)(2,1)S(1)} custom-call(bf16[128,640]{1,0:T(8,128)(2,1)S(1)} %get-tuple-element.88.refs_0_), custom_call_target="tpu_custom_call" | custom-call | tf_op jit(solution)/shard_map/pallas_call | solution.py:415
  135.5 1.4 convolution_convert_fusion.4
  136.9 4.0 %fusion.8 = (bf16[512,512]{1,0:T(8,128)(2,1)}, bf16[512,512]{1,0:T(8,128)(2,1)}) fusion(f32[512,1024]{1,0:T(8,128)} %copy-done.12, bf16[512,640]{1,0:T(8,128)(2,1)S(1)} %bitcast.117, bf16[512,640]{1,0:T(8,128)(2,1)} %all_gather.7), kind=kOutput, calls=%fused_computation.29 | convolution fusion | flops 341835776 | bytes 4456448 | tf_op jit(solution)/shard_map/dot_general | solution.py:674
  141.2 2.7 convolution_convert_fusion.2
  143.8 8.0 %shard_map.277 = f32[128,640]{1,0:T(8,128)S(1)} custom-call(bf16[4,128,640]{2,1,0:T(8,128)(2,1)S(1)} %bitcast.118), custom_call_target="tpu_custom_call" | custom-call | tf_op jit(solution)/shard_map/pallas_call | solution.py:496
  152.4 7.1 %shard_map.278 = bf16[4,128,640]{2,1,0:T(8,128)(2,1)S(1)} custom-call(bf16[128,640]{1,0:T(8,128)(2,1)S(1)} %fusion.36.refs_0_), custom_call_target="tpu_custom_call" | custom-call | tf_op jit(solution)/shard_map/pallas_call | solution.py:415
  161.6 1.9 multiply_cosine_fusion
  165.0 1.2 convolution_convert_fusion.1
  167.5 1.9 convolution_convert_fusion
  170.5 1.1 pad_maximum_fusion.refs_0_
  171.7 11.0 %shard_map.279 = f32[128,1152]{1,0:T(8,128)S(1)} custom-call(bf16[4,128,1152]{2,1,0:T(8,128)(2,1)S(1)} %pad_maximum_fusion.refs_0_), custom_call_target="tpu_custom_call" | custom-call | tf_op jit(solution)/shard_map/pallas_call | solution.py:496
  183.9 1.1 fusion.33
  185.7 1.4 convolution_convert_fusion.6
  187.2 8.2 %shard_map.280 = (bf16[4,128,512]{2,1,0:T(8,128)(2,1)S(1)}, bf16[4,64,640]{2,1,0:T(8,128)(2,1)S(1)}) custom-call(bf16[128,512]{1,0:T(8,128)(2,1)S(1)} %pad_maximum_fusion.11.refs_0_, bf16[4,64,640]{2,1,0:T(8,128)(2,1)S(1)} %bitcast.112), custom_call_target="tpu_custom_call" | custom-call | tf_op jit(solution)/shard_map/pallas_call | solution.py:415
  197.0 5.5 %reduce-scatter.5.cloned.1.call-done.refs_5_ = bf16[64,640]{1,0:T(8,128)(2,1)} async-done(((bf16[512,640]{1,0:T(8,128)(2,1)}), bf16[64,640]{1,0:T(8,128)(2,1)}) %reduce-scatter.5.cloned.1.call-update) | async-done | bytes 81936 | tf_op jit(solution)/shard_map/reduce_scatter | solution.py:799
  202.5 67.1 %reduce-scatter.3.cloned.1.call-done.refs_4_ = bf16[80,1024]{1,0:T(8,128)(2,1)} async-done(((bf16[640,1024]{1,0:T(8,128)(2,1)}), bf16[80,1024]{1,0:T(8,128)(2,1)}) %reduce-scatter.3.cloned.1.call-update) | async-done | bytes 163856 | tf_op jit(solution)/shard_map/reduce_scatter | solution.py:802
  271.4 20.9 %shard_map.281 = (bf16[4,80,256]{2,1,0:T(8,128)(2,1)S(1)}, bf16[4,32,640]{2,1,0:T(8,128)(2,1)S(1)}, bf16[4,80,128]{2,1,0:T(8,128)(2,1)S(1)}, bf16[4,16,384]{2,1,...) custom-call(bf16[8,80,256]{2,1,0:T(8,128)(2,1)S(1)} %bitcast.123, ...), custom_call_target="tpu_custom_call" | custom-call | tf_op jit(solution)/shard_map/pallas_call | solution.py:623
  295.3 1.2 copy.50
  296.4 1.3 reshape.364
  298.3 1.2 copy.51
  (189 shorter events, 30.6 us)
Async XLA Ops:
  7.2 71.3 %copy-start = (bf16[256,640]{1,0:T(8,128)(2,1)S(1)}, bf16[256,640]{1,0:T(8,128)(2,1)}, u32[]{:S(2)}) copy-start(bf16[256,640]{1,0:T(8,128)(2,1)} %param.30) | copy-start | bytes 983044
  7.2 108.0 %all-gather.2.cloned.1.call-start = ((), (), s32[]{:S(2)}) async-start(), calls=%async_computation.2 | async-start | bytes 1474560 | tf_op jit(solution)/shard_map/all_gather | solution.py:712
  7.2 3.7 %copy-start.34 = (bf16[80]{0:T(256)(128)(2,1)S(1)}, bf16[80]{0:T(256)(128)(2,1)}, u32[]{:S(2)}) copy-start(bf16[80]{0:T(256)(128)(2,1)} %param.19) | copy-start | bytes 484
  7.3 3.7 %copy-start.35 = (bf16[80]{0:T(256)(128)(2,1)S(1)}, bf16[80]{0:T(256)(128)(2,1)}, u32[]{:S(2)}) copy-start(bf16[80]{0:T(256)(128)(2,1)} %param.26) | copy-start | bytes 484
  7.3 3.7 %copy-start.36 = (bf16[80]{0:T(256)(128)(2,1)S(1)}, bf16[80]{0:T(256)(128)(2,1)}, u32[]{:S(2)}) copy-start(bf16[80]{0:T(256)(128)(2,1)} %param.27) | copy-start | bytes 484
  7.3 3.7 %copy-start.37 = (bf16[80]{0:T(256)(128)(2,1)S(1)}, bf16[80]{0:T(256)(128)(2,1)}, u32[]{:S(2)}) copy-start(bf16[80]{0:T(256)(128)(2,1)} %param.31) | copy-start | bytes 484
  7.3 3.7 %copy-start.38 = (bf16[32]{0:T(256)(128)(2,1)S(1)}, bf16[32]{0:T(256)(128)(2,1)}, u32[]{:S(2)}) copy-start(bf16[32]{0:T(256)(128)(2,1)} %param.23) | copy-start | bytes 196
  7.3 3.7 %copy-start.39 = (bf16[32]{0:T(256)(128)(2,1)S(1)}, bf16[32]{0:T(256)(128)(2,1)}, u32[]{:S(2)}) copy-start(bf16[32]{0:T(256)(128)(2,1)} %param.24) | copy-start | bytes 196
  7.3 5.4 %copy-start.31 = (bf16[80,256]{1,0:T(8,128)(2,1)S(1)}, bf16[80,256]{1,0:T(8,128)(2,1)}, u32[]{:S(2)}) copy-start(bf16[80,256]{1,0:T(8,128)(2,1)} %param.22) | copy-start | bytes 122884
  7.3 5.4 %copy-start.32 = (bf16[80,256]{1,0:T(8,128)(2,1)S(1)}, bf16[80,256]{1,0:T(8,128)(2,1)}, u32[]{:S(2)}) copy-start(bf16[80,256]{1,0:T(8,128)(2,1)} %param.21) | copy-start | bytes 122884
  10.2 34.5 %copy-start.11 = (bf16[1,128,640]{2,1,0:T(8,128)(2,1)S(1)}, bf16[1,128,640]{2,1,0:T(8,128)(2,1)}, u32[]{:S(2)}) copy-start(bf16[1,128,640]{2,1,0:T(8,128)(2,1)} %param.16) | copy-start | bytes 491524
  10.9 191.6 %reduce-scatter.5.cloned.1.call-start = ((), (), s32[]{:S(2)}) async-start(), calls=%async_computation.4 | async-start | bytes 737280 | tf_op jit(solution)/shard_map/reduce_scatter | solution.py:799
  11.9 33.0 %copy-start.33 = (s32[1,128]{1,0:T(1,128)S(1)}, s32[1,128]{1,0:T(1,128)}, u32[]{:S(2)}) copy-start(s32[1,128]{1,0:T(1,128)} %param.17) | copy-start | bytes 1540
  56.7 3.6 %copy-start.3 = (f32[512,768]{1,0:T(8,128)}, f32[512,768]{1,0:T(8,128)S(1)}, u32[]{:S(2)}) copy-start(f32[512,768]{1,0:T(8,128)S(1)} %fusion.82) | copy-start | bytes 4718596
  61.1 56.4 %copy-start.16 = (bf16[512,256]{1,0:T(8,128)(2,1)}, bf16[512,256]{1,0:T(8,128)(2,1)S(1)}, u32[]{:S(2)}) copy-start(bf16[512,256]{1,0:T(8,128)(2,1)S(1)} %convolution_convert_fusion.9) | copy-start | bytes 786436
  117.5 2.1 copy-start.12
  117.5 1.6 copy-start.19
  119.1 8.0 %copy-start.14 = (bf16[1,128,640]{2,1,0:T(8,128)(2,1)S(1)}, bf16[1,128,640]{2,1,0:T(8,128)(2,1)}, u32[]{:S(2)}) copy-start(bf16[1,128,640]{2,1,0:T(8,128)(2,1)} %param.18) | copy-start | bytes 491524
  140.9 128.6 %reduce-scatter.3.cloned.1.call-start = ((), (), s32[]{:S(2)}) async-start(), calls=%async_computation.3 | async-start | bytes 1474560 | tf_op jit(solution)/shard_map/reduce_scatter | solution.py:802
  143.8 8.1 %copy-start.15 = (bf16[1,128,640]{2,1,0:T(8,128)(2,1)S(1)}, bf16[1,128,640]{2,1,0:T(8,128)(2,1)}, u32[]{:S(2)}) copy-start(bf16[1,128,640]{2,1,0:T(8,128)(2,1)} %param.18) | copy-start | bytes 491524
  152.3 8.0 %copy-start.8 = (f32[128,640]{1,0:T(8,128)}, f32[128,640]{1,0:T(8,128)S(1)}, u32[]{:S(2)}) copy-start(f32[128,640]{1,0:T(8,128)S(1)} %get-tuple-element.70) | copy-start | bytes 983044
  152.3 7.6 %copy-start.4 = (f32[512,768]{1,0:T(8,128)S(1)}, f32[512,768]{1,0:T(8,128)}, u32[]{:S(2)}) copy-start(f32[512,768]{1,0:T(8,128)} %copy-done.3) | copy-start | bytes 4718596
  152.3 7.6 %copy-start.7 = (f32[512,512]{0,1:T(8,128)S(1)}, f32[512,512]{0,1:T(8,128)}, u32[]{:S(2)}) copy-start(f32[512,512]{0,1:T(8,128)} %copy-done.6) | copy-start | bytes 3145732
  161.6 2.2 copy-start.24
  161.6 2.2 copy-start.26
  165.0 2.3 copy-start.17
  171.7 12.0 %copy-start.13 = (f32[512,256]{1,0:T(8,128)S(1)}, f32[512,256]{1,0:T(8,128)}, u32[]{:S(2)}) copy-start(f32[512,256]{1,0:T(8,128)} %get-tuple-element.75) | copy-start | bytes 1572868
  182.7 2.3 copy-start.21
  185.0 2.2 copy-start.22
  185.7 10.1 %copy-start.9 = (f32[128,640]{1,0:T(8,128)S(1)}, f32[128,640]{1,0:T(8,128)}, u32[]{:S(2)}) copy-start(f32[128,640]{1,0:T(8,128)} %copy-done.8) | copy-start | bytes 983044
  185.7 10.1 %copy-start.20 = (f32[128,640]{1,0:T(8,128)S(1)}, f32[128,640]{1,0:T(8,128)}, u32[]{:S(2)}) copy-start(f32[128,640]{1,0:T(8,128)} %get-tuple-element.114) | copy-start | bytes 983044
  187.1 9.5 %copy-start.18 = (bf16[512,256]{1,0:T(8,128)(2,1)S(1)}, bf16[512,256]{1,0:T(8,128)(2,1)}, u32[]{:S(2)}) copy-start(bf16[512,256]{1,0:T(8,128)(2,1)} %copy-done.17) | copy-start | bytes 786436
  (13 other events, 12.1 us)
Sparse Core Ops, SparseCore 0:
  11.0 51.1 all-gather.1
  141.1 61.3 reduce-scatter.4
  206.3 63.2 reduce-scatter.2

commit v3 on v2

--- a/solution.py
+++ b/solution.py
@@ -330,179 +330,172 @@
     return dict(device_id={axis: index}, device_id_type=pl.DeviceIdType.MESH)
 
 
-def greet(axis, indices):
-    barrier = pltpu.get_barrier_semaphore()
-    for index in indices:
-        pl.semaphore_signal(barrier, inc=1, **peer_of(axis, index))
-    pl.semaphore_wait(barrier, len(indices))
-
-
-def gather_kernel(axis, n, count, swaps, *refs):
-    every = count + swaps
-    ins, outs = refs[:every], refs[every : 2 * every]
-    send, recv = refs[2 * every :]
-    me = lax.axis_index(axis)
-    outer, inner = lax.div(me, 2), lax.rem(me, 2)
-    span = n // 2
-    twin = outer * 2 + (1 - inner)
-
-    def ahead(step):
-        return lax.rem(outer + step, span) * 2 + inner
-
-    def behind(step):
-        return lax.rem(outer + span - step, span)
-
-    if swaps:
-        greet(axis, [lax.rem(me + step, n) for step in range(1, n)])
-    else:
-        greet(axis, [twin] + [ahead(step) for step in range(1, span)])
-
-    def trade(i, step, slot):
-        target = lax.rem(me + step, n)
-        return pltpu.make_async_remote_copy(
-            src_ref=ins[i].at[target],
-            dst_ref=outs[i].at[slot],
-            send_sem=send.at[i, step - 1],
-            recv_sem=recv.at[i, step - 1],
-            **peer_of(axis, target),
-        )
-
-    def copy(i, source, slot, lane, target):
+class Piece:
+    def __init__(self, axis, n, source, result, slots, send, recv):
+        self.axis, self.n, self.source, self.result = axis, n, source, result
+        self.slots, self.send, self.recv = slots, send, recv
+        self.me = lax.axis_index(axis)
+        self.outer, self.inner = lax.div(self.me, 2), lax.rem(self.me, 2)
+        self.span = n // 2
+        self.twin = self.outer * 2 + (1 - self.inner)
+
+    def ahead(self, step):
+        return lax.rem(self.outer + step, self.span)
+
+    def behind(self, step):
+        return lax.rem(self.outer + self.span - step, self.span)
+
+    def copy(self, source, target_ref, lane, target):
         return pltpu.make_async_remote_copy(
             src_ref=source,
-            dst_ref=outs[i].at[slot],
-            send_sem=send.at[i, lane],
-            recv_sem=recv.at[i, lane],
-            **peer_of(axis, target),
+            dst_ref=target_ref,
+            send_sem=self.send.at[lane],
+            recv_sem=self.recv.at[lane],
+            **peer_of(self.axis, target),
         )
 
-    for i in range(count):
-        for step in range(1, span):
-            copy(i, ins[i], me, step, ahead(step)).start()
-        copy(i, ins[i], me, 0, twin).start()
-    for i in range(count, every):
-        for step in range(1, n):
-            trade(i, step, me).start()
-    for i in range(count):
-        outs[i][me] = ins[i][...]
-    for i in range(count, every):
-        outs[i][me] = ins[i][me]
-    for i in range(count):
-        for step in range(1, span):
-            slot = behind(step) * 2 + inner
-            copy(i, ins[i], slot, step, twin).wait_recv()
-            copy(i, outs[i].at[slot], slot, span - 1 + step, twin).start()
-    for i in range(count):
-        copy(i, ins[i], twin, 0, twin).wait_recv()
-        for step in range(1, span):
-            slot = behind(step) * 2 + (1 - inner)
-            copy(i, ins[i], slot, span - 1 + step, twin).wait_recv()
-        for lane in range(2 * span - 1):
-            copy(i, ins[i], me, lane, twin).wait_send()
-    for i in range(count, every):
-        for step in range(1, n):
-            trade(i, step, lax.rem(me + n - step, n)).wait_recv()
-        for step in range(1, n):
-            trade(i, step, me).wait_send()
-
-
-def gather(axis, n, key, *arrays, swapped=()):
-    kept = len(arrays)
-    shapes = [(n,) + a.shape for a in arrays] + [a.shape for a in swapped]
-    arrays = arrays + swapped
-    count = len(arrays)
+
+class Gather(Piece):
+    def out(self, source, slot, lane, target):
+        return self.copy(source, self.result.at[slot], lane, target)
+
+    def begin(self):
+        for step in range(1, self.span):
+            self.out(self.source, self.me, step, self.ahead(step) * 2 + self.inner).start()
+        self.out(self.source, self.me, 0, self.twin).start()
+
+    def own(self):
+        self.result[self.me] = self.source[...]
+
+    def middle(self):
+        for step in range(1, self.span):
+            slot = self.behind(step) * 2 + self.inner
+            self.out(self.source, slot, step, self.twin).wait_recv()
+            self.out(self.result.at[slot], slot, self.span - 1 + step, self.twin).start()
+
+    def end(self):
+        self.out(self.source, self.twin, 0, self.twin).wait_recv()
+        for step in range(1, self.span):
+            slot = self.behind(step) * 2 + (1 - self.inner)
+            self.out(self.source, slot, self.span - 1 + step, self.twin).wait_recv()
+        for lane in range(2 * self.span - 1):
+            self.out(self.source, self.me, lane, self.twin).wait_send()
+
+
+class Swap(Piece):
+    def trade(self, step, slot):
+        target = lax.rem(self.me + step, self.n)
+        return self.copy(self.source.at[target], self.result.at[slot], step, target)
+
+    def begin(self):
+        for step in range(1, self.n):
+            self.trade(step, self.me).start()
+
+    def own(self):
+        self.result[self.me] = self.source[self.me]
+
+    def middle(self):
+        pass
+
+    def end(self):
+        for step in range(1, self.n):
+            self.trade(step, lax.rem(self.me + self.n - step, self.n)).wait_recv()
+        for step in range(1, self.n):
+            self.trade(step, self.me).wait_send()
+
+
+class Sum(Piece):
+    def to_twin(self, step):
+        block = self.source.at[self.ahead(step) * 2 + (1 - self.inner)]
+        return self.copy(block, self.slots[0].at[step], step, self.twin)
+
+    def to_owner(self, step):
+        return self.copy(
+            self.slots[1].at[step],
+            self.slots[2].at[step],
+            self.span + step,
+            self.ahead(step) * 2 + self.inner,
+        )
+
+    def begin(self):
+        for step in list(range(1, self.span)) + [0]:
+            self.to_twin(step).start()
+
+    def own(self):
+        pass
+
+    def middle(self):
+        from_twin, paired = self.slots[:2]
+        for step in range(1, self.span):
+            self.to_twin(step).wait_recv()
+            mine = self.source[self.ahead(step) * 2 + self.inner].astype(jnp.float32)
+            paired[step] = (mine + from_twin[step].astype(jnp.float32)).astype(paired.dtype)
+            self.to_owner(step).start()
+
+    def end(self):
+        self.to_twin(0).wait_recv()
+        total = self.source[self.me].astype(jnp.float32) + self.slots[0][0].astype(jnp.float32)
+        for step in range(1, self.span):
+            self.to_owner(step).wait_recv()
+            total = total + self.slots[2][step].astype(jnp.float32)
+        self.result[...] = total.astype(self.result.dtype)
+        for step in range(self.span):
+            self.to_twin(step).wait_send()
+        for step in range(1, self.span):
+            self.to_owner(step).wait_send()
+
+
+def exchange_kernel(plan, *refs):
+    count = len(plan)
+    send, recv = refs[-2:]
+    slots = list(refs[2 * count : -2])
+    pieces = []
+    for i, (kind, axis, n) in enumerate(plan):
+        own_slots = [slots.pop(0) for _ in range(3)] if kind is Sum else []
+        pieces.append(kind(axis, n, refs[i], refs[count + i], own_slots, send.at[i], recv.at[i]))
+    barrier = pltpu.get_barrier_semaphore()
+    heard = 0
+    for axis, n in sorted({(axis, n) for _, axis, n in plan}):
+        first = [piece for piece in pieces if piece.axis == axis][0]
+        if any(kind is Swap and name == axis for kind, name, _ in plan):
+            peers = [lax.rem(first.me + step, n) for step in range(1, n)]
+        else:
+            peers = [first.twin]
+            peers += [first.ahead(step) * 2 + first.inner for step in range(1, n // 2)]
+        for peer in peers:
+            pl.semaphore_signal(barrier, inc=1, **peer_of(axis, peer))
+        heard += len(peers)
+    pl.semaphore_wait(barrier, heard)
+    for piece in pieces:
+        piece.begin()
+    for piece in pieces:
+        piece.own()
+    for piece in pieces:
+        piece.middle()
+    for piece in pieces:
+        piece.end()
+
+
+def exchange(key, *pieces):
+    plan = [(kind, axis, lax.axis_size(axis)) for kind, axis, _, _ in pieces]
+    arrays = [piece[2] for piece in pieces]
     spec = pl.BlockSpec(memory_space=pltpu.VMEM)
+    shapes, slots = [], []
+    for (kind, _, n), (_, _, array, kept) in zip(plan, pieces):
+        if kind is Gather:
+            shapes.append(jax.ShapeDtypeStruct((n,) + array.shape, kept))
+        elif kind is Swap:
+            shapes.append(jax.ShapeDtypeStruct(array.shape, kept))
+        else:
+            shapes.append(jax.ShapeDtypeStruct(array.shape[1:], kept))
+            slots += [pltpu.VMEM((n // 2,) + array.shape[1:], array.dtype)] * 3
+    lanes = max(n for _, _, n in plan)
     return pl.pallas_call(
-        functools.partial(gather_kernel, axis, n, kept, len(swapped)),
-        out_shape=[jax.ShapeDtypeStruct(shape, a.dtype) for shape, a in zip(shapes, arrays)],
-        in_specs=[spec] * count,
-        out_specs=[spec] * count,
-        scratch_shapes=[
-            pltpu.SemaphoreType.DMA((count, n - 1)),
-            pltpu.SemaphoreType.DMA((count, n - 1)),
-        ],
-        compiler_params=pltpu.CompilerParams(
-            collective_id=key, has_side_effects=True, vmem_limit_bytes=VMEM_BYTES
-        ),
-    )(*arrays)
-
-
-def add_scatter_kernel(axis, n, count, *refs):
-    ins, outs = refs[:count], refs[count : 2 * count]
-    from_twin, paired, landed = (
-        refs[2 * count : 3 * count],
-        refs[3 * count : 4 * count],
-        refs[4 * count : 5 * count],
-    )
-    send, recv = refs[5 * count :]
-    me = lax.axis_index(axis)
-    outer, inner = lax.div(me, 2), lax.rem(me, 2)
-    span = n // 2
-    twin = outer * 2 + (1 - inner)
-    f32 = jnp.float32
-
-    def ahead(step):
-        return lax.rem(outer + step, span)
-
-    greet(axis, [twin] + [ahead(step) * 2 + inner for step in range(1, span)])
-
-    def to_twin(i, step):
-        return pltpu.make_async_remote_copy(
-            src_ref=ins[i].at[ahead(step) * 2 + (1 - inner)],
-            dst_ref=from_twin[i].at[step],
-            send_sem=send.at[i, step],
-            recv_sem=recv.at[i, step],
-            **peer_of(axis, twin),
-        )
-
-    def to_owner(i, step):
-        return pltpu.make_async_remote_copy(
-            src_ref=paired[i].at[step],
-            dst_ref=landed[i].at[step],
-            send_sem=send.at[i, span + step],
-            recv_sem=recv.at[i, span + step],
-            **peer_of(axis, ahead(step) * 2 + inner),
-        )
-
-    order = list(range(1, span)) + [0]
-    for i in range(count):
-        for step in order:
-            to_twin(i, step).start()
-    for i in range(count):
-        for step in range(1, span):
-            to_twin(i, step).wait_recv()
-            paired[i][step] = (
-                ins[i][ahead(step) * 2 + inner].astype(f32) + from_twin[i][step].astype(f32)
-            ).astype(paired[i].dtype)
-            to_owner(i, step).start()
-    for i in range(count):
-        to_twin(i, 0).wait_recv()
-        total = ins[i][me].astype(f32) + from_twin[i][0].astype(f32)
-        for step in range(1, span):
-            to_owner(i, step).wait_recv()
-            total = total + landed[i][step].astype(f32)
-        outs[i][...] = total.astype(outs[i].dtype)
-    for i in range(count):
-        for step in range(span):
-            to_twin(i, step).wait_send()
-        for step in range(1, span):
-            to_owner(i, step).wait_send()
-
-
-def add_scatter(axis, n, key, out_type, *arrays):
-    count = len(arrays)
-    spec = pl.BlockSpec(memory_space=pltpu.VMEM)
-    slots = [pltpu.VMEM((n // 2,) + a.shape[1:], a.dtype) for a in arrays]
-    return pl.pallas_call(
-        functools.partial(add_scatter_kernel, axis, n, count),
-        out_shape=[jax.ShapeDtypeStruct(a.shape[1:], out_type) for a in arrays],
-        in_specs=[spec] * count,
-        out_specs=[spec] * count,
-        scratch_shapes=slots * 3
-        + [
-            pltpu.SemaphoreType.DMA((count, n)),
-            pltpu.SemaphoreType.DMA((count, n)),
-        ],
+        functools.partial(exchange_kernel, plan),
+        out_shape=shapes,
+        in_specs=[spec] * len(arrays),
+        out_specs=[spec] * len(arrays),
+        scratch_shapes=slots + [pltpu.SemaphoreType.DMA((len(plan), lanes))] * 2,
         compiler_params=pltpu.CompilerParams(
             collective_id=key, has_side_effects=True, vmem_limit_bytes=VMEM_BYTES
         ),
@@ -667,6 +660,7 @@
     hidden_row = w_down.shape[0] // ways
     out_row = w_output.shape[0] // ways
     head_share = query_norm.shape[0]
+    hidden_cols = owners * hidden_row
     inputs = tokens.reshape(rows, width).astype(f32)
     grad_out = cotangent.reshape(rows, width).astype(f32)
 
@@ -709,24 +703,15 @@
         axis=0,
     )
     hidden_cols = owners * hidden_row
-    wgu_part = lax.all_gather(
-        jnp.concatenate([hidden_part(w_gate), hidden_part(w_up)], axis=1),
-        "fsdp",
-        axis=0,
-        tiled=True,
-    )
-    wd_part = lax.all_gather(
-        lax.dynamic_slice_in_dim(w_down, part * hidden_row, hidden_row, 0),
-        "fsdp",
-        axis=0,
-        tiled=True,
-    )
-    attn_all, wo_rows = gather(
-        "fsdp",
-        owners,
+    attn_all, wo_rows = exchange(
         0,
-        attn_pack,
-        lax.dynamic_slice_in_dim(w_output, part * out_row, out_row, 0),
+        (Gather, "fsdp", attn_pack, bf16),
+        (
+            Gather,
+            "fsdp",
+            lax.dynamic_slice_in_dim(w_output, part * out_row, out_row, 0),
+            bf16,
+        ),
     )
     gains = attn_all[:, shard, :gain_size].astype(f32)
 
@@ -739,14 +724,14 @@
     w_qkv = attn_all[:, :shard].reshape(width, 3 * HD)
     wq_head, wk_full, wv_full = (w_qkv[:, i * HD : (i + 1) * HD] for i in range(3))
     attn_in = rms_gain(inputs, g_attn).astype(bf16)
-    attn_seq, place_all, wo_head = gather(
-        "ctx",
-        ways,
+    attn_seq, place_all, wo_head, wg_all = exchange(
         2,
-        attn_in,
-        jnp.broadcast_to(positions.reshape(1, rows), (8, rows)),
-        swapped=(wo_rows.reshape(ways, owners // ways * out_row, width),),
-    )
+        (Gather, "ctx", attn_in, bf16),
+        (Gather, "ctx", jnp.broadcast_to(positions.reshape(1, rows), (8, rows)), jnp.int32),
+        (Swap, "ctx", wo_rows.reshape(ways, owners // ways * out_row, width), bf16),
+        (Gather, "fsdp", hidden_part(w_gate), bf16),
+    )
+    wg_part = wg_all.reshape(width, hidden_cols)
     wo_head = (
         wo_head.reshape(ways, owners // ways, out_row, width)
         .transpose(1, 0, 2, 3)
@@ -773,40 +758,58 @@
     prob_low = prob_rows.astype(bf16)
     att_low = nn(prob_low, v_low).astype(bf16)
 
-    def own_sum(key, value):
-        return add_scatter(
-            "ctx", ways, key, f32, value.astype(bf16).reshape(ways, rows, value.shape[1])
-        )[0]
-
-    def whole(key, value):
-        return gather("ctx", ways, key, value)[0].reshape(seq, value.shape[1])
-
-    branch = own_sum(3, nn(att_low, wo_head))
+    def by_rows(value):
+        return value.astype(bf16).reshape(ways, rows, value.shape[1])
+
+    def blocks(value):
+        return value.astype(bf16).reshape(owners, value.shape[0] // owners, value.shape[1])
+
+    branch, wu_all = exchange(
+        3,
+        (Sum, "ctx", by_rows(nn(att_low, wo_head)), f32),
+        (Gather, "fsdp", hidden_part(w_up), bf16),
+    )
+    wu_part = wu_all.reshape(width, hidden_cols)
     hidden_res = inputs + rms_gain(branch, g_post)
-    ffn_seq = whole(4, rms_gain(hidden_res, g_ffn).astype(bf16))
-    gate_up = nn(ffn_seq, wgu_part)
-    gate_proj, up_proj = gate_up[:, :hidden_cols], gate_up[:, hidden_cols:]
+    ffn_seq, wd_all = exchange(
+        4,
+        (Gather, "ctx", rms_gain(hidden_res, g_ffn).astype(bf16), bf16),
+        (
+            Gather,
+            "fsdp",
+            lax.dynamic_slice_in_dim(w_down, part * hidden_row, hidden_row, 0),
+            bf16,
+        ),
+    )
+    ffn_seq = ffn_seq.reshape(seq, width)
+    wd_part = wd_all.reshape(hidden_cols, width)
+    gate_proj = nn(ffn_seq, wg_part)
+    up_proj = nn(ffn_seq, wu_part)
     mixed_low = gated_gelu(gate_proj, up_proj).astype(bf16)
-    down_out = own_sum(5, nn(mixed_low, wd_part))
+    (down_out,) = exchange(5, (Sum, "ctx", by_rows(nn(mixed_low, wd_part)), f32))
     layer_out = hidden_res + rms_gain(down_out, g_ffn_post)
 
     d_down, d_ffn_post = jax.vjp(rms_gain, down_out, g_ffn_post)[1](grad_out)
-    d_down_seq = whole(6, d_down.astype(bf16))
+    d_down_seq = exchange(6, (Gather, "ctx", d_down.astype(bf16), bf16))[0].reshape(seq, width)
     d_mixed = nt(d_down_seq, wd_part)
     d_gate, d_up = jax.vjp(gated_gelu, gate_proj, up_proj)[1](d_mixed)
-    d_gate_up = jnp.concatenate([d_gate.astype(bf16), d_up.astype(bf16)], axis=1)
-    d_ffn_in = own_sum(7, nt(d_gate_up, wgu_part))
-    wd_g = lax.psum_scatter(
-        tn(mixed_low, d_down_seq).astype(bf16), "fsdp", scatter_dimension=0, tiled=True
-    )
-    wgu_g = lax.psum_scatter(
-        tn(ffn_seq, d_gate_up).astype(bf16), "fsdp", scatter_dimension=0, tiled=True
+    d_gate_low = d_gate.astype(bf16)
+    d_up_low = d_up.astype(bf16)
+    d_ffn_in, wd_g = exchange(
+        7,
+        (Sum, "ctx", by_rows(nt(d_gate_low, wg_part) + nt(d_up_low, wu_part)), f32),
+        (Sum, "fsdp", blocks(tn(mixed_low, d_down_seq)), bf16),
     )
     d_hidden_part, d_ffn_norm = jax.vjp(rms_gain, hidden_res, g_ffn)[1](d_ffn_in)
     d_hidden = grad_out + d_hidden_part
 
     d_branch, d_post = jax.vjp(rms_gain, branch, g_post)[1](d_hidden)
-    d_branch_seq = whole(8, d_branch.astype(bf16))
+    d_branch_seq, wg_g = exchange(
+        8,
+        (Gather, "ctx", d_branch.astype(bf16), bf16),
+        (Sum, "fsdp", blocks(tn(ffn_seq, d_gate_low)), bf16),
+    )
+    d_branch_seq = d_branch_seq.reshape(seq, width)
     grad_w_output = tn(att_low, d_branch_seq)
     d_att = nt(d_branch_seq, wo_head).astype(bf16)
     d_values = tn(prob_low, d_att)
@@ -819,7 +822,16 @@
         lambda values, gain_vec: turned_norm(values, gain_vec, cosine, sine_table), q_pre, g_query
     )[1](d_queries)
     dq_low = d_q_pre.astype(bf16)
-    sums = own_sum(9, jnp.concatenate([nt(dq_low, wq_head), d_keys, d_values], axis=1))
+    sums, wu_g = exchange(
+        9,
+        (
+            Sum,
+            "ctx",
+            by_rows(jnp.concatenate([nt(dq_low, wq_head), d_keys, d_values], axis=1)),
+            f32,
+        ),
+        (Sum, "fsdp", blocks(tn(ffn_seq, d_up_low)), bf16),
+    )
     own_cos = lax.dynamic_slice_in_dim(cosine, part * rows, rows, 0)
     own_sin = lax.dynamic_slice_in_dim(sine_table, part * rows, rows, 0)
     own_k = lax.dynamic_slice_in_dim(k_pre, part * rows, rows, 0)
@@ -828,23 +840,24 @@
     )[1](sums[:, width : width + HD])
     dkv_low = jnp.concatenate([d_k_pre, sums[:, width + HD :]], axis=1).astype(bf16)
     d_attn_in = sums[:, :width] + nt(dkv_low, w_qkv[:, HD:])
-    dkv_seq, grad_wo_rows = gather(
-        "ctx",
-        ways,
+    dkv_seq, grad_wo_rows, wq_g = exchange(
         10,
-        dkv_low,
-        swapped=(
+        (Gather, "ctx", dkv_low, bf16),
+        (
+            Swap,
+            "ctx",
             grad_w_output.astype(bf16)
             .reshape(owners // ways, ways, out_row, width)
             .transpose(1, 0, 2, 3)
             .reshape(ways, owners // ways * out_row, width),
+            bf16,
         ),
+        (Sum, "fsdp", blocks(tn(attn_seq, dq_low)), bf16),
     )
     dkv_seq = dkv_seq.reshape(seq, 2 * HD)
     grad_wo_rows = grad_wo_rows.reshape(owners, out_row, width)
     d_inputs_part, d_attn_norm = jax.vjp(rms_gain, inputs, g_attn)[1](d_attn_in)
     d_tokens = d_hidden + d_inputs_part
-    grad_w_query = tn(attn_seq, dq_low)
     dkv_cols = 2 * HD // ways
     grad_w_kv = tn(attn_seq, lax.dynamic_slice_in_dim(dkv_seq, part * dkv_cols, dkv_cols, 1))
 
@@ -857,15 +870,12 @@
     )
     gain_grads = jnp.pad(gain_grads[:, None], ((0, 0), (0, 15), (0, 0)))
 
-    def blocks(value):
-        return value.astype(bf16).reshape(owners, value.shape[0] // owners, value.shape[1])
-
-    wq_g, wo_g, wkv_g, gain_g, wgu_g, wd_g = finish(
+    wo_g, wkv_g, gain_g, wg_g, wu_g, wd_g, wq_g = finish(
         owners,
         ways,
         12,
-        [blocks(grad_w_query), grad_wo_rows, blocks(grad_w_kv), gain_grads.astype(bf16)],
-        [wgu_g, wd_g],
+        [grad_wo_rows, blocks(grad_w_kv), gain_grads.astype(bf16)],
+        [wg_g, wu_g, wd_g, wq_g],
     )
     gain_sum = jnp.sum(gain_g[:, 0].astype(f32), axis=0)
     ends = [shard * i for i in range(1, 5)] + [4 * shard + head_share]
@@ -887,8 +897,8 @@
         wo_g.reshape(ways * out_row, width).astype(f32),
         t_post,
         t_ffn,
-        hidden_whole(wgu_g[:, :, :hidden_cols]).astype(f32),
-        hidden_whole(wgu_g[:, :, hidden_cols:]).astype(f32),
+        hidden_whole(wg_g).astype(f32),
+        hidden_whole(wu_g).astype(f32),
         wd_g.reshape(ways * hidden_row, width).astype(f32),
         t_ffn_post,
     )

time: 311 us -> 225 us (0.72)
  waiting for transfers between devices: 72.6 us -> 0 us
  blocking collectives: 36.6 us -> 0 us
  Pallas kernels: 125 us -> 157 us
  between operations: 14.7 us -> 1.51 us
  other arithmetic: 15.6 us -> 21.5 us
  matrix products: 23.7 us -> 18.3 us
  local copies, waits for them, and re-layouts: 20.7 us -> 25.4 us
    reduce_scatter x2 -> x0, waiting for transfers between devices: 72.6 us -> none  [the longest x1 67.1 us: split_body(): lax.psum_scatter(tn(ffn_seq, d_gate_up).astype(bf16), 'fsdp', scatter_dim...]
    all_gather x1 -> x0, blocking collectives: 36.6 us -> none  [split_body(): lax.all_gather(lax.dynamic_slice_in_dim(w_down, part * hidden_row, hidden...]
    pallas_call x10, Pallas kernels: 105 us -> 141 us  [exchange(): pl.pallas_call(functools.partial(exchange_kernel, plan), out_shape=shapes...]
    dot_general x20 -> x23, matrix products: 23.7 us -> 18.3 us  [mul(): lax.dot_general(left, right, (dims, ((), ())), preferred_element_type=f32)]
    pallas_call x1, Pallas kernels: 20.9 us -> 16.8 us  [finish(): pl.pallas_call(functools.partial(finish_kernel, owners, ways, sums, count...]
    concatenate x1, local copies, waits for them, and re-layouts: 0.1 us -> 4.16 us  [split_body(): jnp.concatenate([attn_norm, attn_post_norm, ffn_norm, ffn_post_norm, quer...]
    unnamed x89 -> x73, local copies, waits for them, and re-layouts: 10.7 us -> 11.1 us
  transfers between devices with their start and end apart: 3 -> 0, of which waited for: 2 -> 0; matrix products, arithmetic and copies ran while one was open for 10% -> 0% of each run, Pallas kernels for 29% -> 0%
where the time goes in v3:
time: 225 us; the launch traced here: 224 us
  Pallas kernels  157 us (70%)
  local copies, waits for them, and re-layouts  25.4 us (11%)
  other arithmetic  21.5 us (10%)
  matrix products  18.3 us (8%)
    pallas_call x10, Pallas kernels, exchange(): pl.pallas_call(functools.partial(exchange_kernel, plan), out_shape=shapes...  141 us
    dot_general x23, matrix products, mul(): lax.dot_general(left, right, (dims, ((), ())), preferred_element_type=f32)  18.3 us
    pallas_call x1, Pallas kernels, finish(): pl.pallas_call(functools.partial(finish_kernel, owners, ways, sums, count...  16.8 us
    unnamed x73, local copies, waits for them, and re-layouts  11.1 us

profile of v3, /device:TPU:0, one launch (start us, length us, event | category | flops | bytes accessed | tf_op | source)
XLA Modules:
  0.0 224.2 jit_solution(13182131139544445098)
XLA Ops:
  0.7 4.2 %concatenate.37 = bf16[384]{0:T(512)(128)(2,1)S(1)} concatenate(bf16[80]{0:T(256)(128)(2,1)} %param.19, bf16[80]{0:T(256)(128)(2,1)} %param.26, bf16[80]{0:T(256)(128)(2,1)} %param.27, bf16[80]{0:T(256)(128)(2,1)} %param.31, bf16[32]{0:T(256)(128)(2,1)} %param.23, bf16[32]{0:T(256)(128)(2,1)} %param.24), dimensions={0} | concatenate | bytes 1536 | tf_op jit(solution)/shard_map/concatenate | solution.py:692
  7.2 28.0 %shard_map.271 = (bf16[8,96,768]{2,1,0:T(8,128)(2,1)S(1)}, bf16[8,32,640]{2,1,0:T(8,128)(2,1)S(1)}) custom-call(bf16[96,768]{1,0:T(8,128)(2,1)S(1)} %fusion.59.refs_0_, bf16[32,640]{1,0:T(8,128)(2,1)S(1)} %constant_dynamic-slice_fusion.3.refs_1_), custom_call_target="tpu_custom_call" | custom-call | tf_op jit(solution)/shard_map/pallas_call | solution.py:493
  35.5 1.0 fusion.41
  36.6 1.0 fusion.33.refs_0_
  38.6 1.2 copy.36
  41.6 16.4 %shard_map.272 = (bf16[4,128,640]{2,1,0:T(8,128)(2,1)S(1)}, s32[4,8,128]{2,1,0:T(8,128)S(1)}, bf16[4,64,640]{2,1,0:T(8,128)(2,1)S(1)}, bf16[8,80,512]{2,1,0:T(8,128)(2,1)S(1)}) custom-call(bf16[128,640]{1,0:T(8,128)(2,1)S(1)} %fusion.33.refs_0_, s32[8,128]{1,0:T(8,128)S(1)} %broadcast_in_dim.27.refs_1_, bf16[4,64,640]{2,1,0:T(8,128)(2,1)S(1)} %bitcast.145, ...), custom_call_target="tpu_custom_call" | custom-call | tf_op jit(solution)/shard_map/pallas_call | solution.py:493
  58.1 1.9 fusion.81
  60.2 1.4 multiply_reduce_fusion.4
  61.7 2.1 fusion.75
  63.9 1.4 fusion.46
  66.3 1.6 convolution_convert_fusion.9
  69.1 13.9 %shard_map.273 = (f32[128,640]{1,0:T(8,128)S(1)}, bf16[8,80,512]{2,1,0:T(8,128)(2,1)S(1)}) custom-call(bf16[4,128,640]{2,1,0:T(8,128)(2,1)S(1)} %bitcast.124, bf16[80,512]{1,0:T(8,128)(2,1)S(1)} %copy.51.refs_1_), custom_call_target="tpu_custom_call" | custom-call | tf_op jit(solution)/shard_map/pallas_call | solution.py:493
  84.4 14.0 %shard_map.274 = (bf16[4,128,640]{2,1,0:T(8,128)(2,1)S(1)}, bf16[8,64,640]{2,1,0:T(8,128)(2,1)S(1)}) custom-call(bf16[128,640]{1,0:T(8,128)(2,1)S(1)} %multiply_convert_fusion.3.refs_0_, bf16[64,640]{1,0:T(8,128)(2,1)S(1)} %constant_dynamic-slice_fusion.refs_1_), custom_call_target="tpu_custom_call" | custom-call | tf_op jit(solution)/shard_map/pallas_call | solution.py:493
  99.1 1.6 multiply_convert_fusion.2
  101.3 6.6 %shard_map.275 = f32[128,640]{1,0:T(8,128)S(1)} custom-call(bf16[4,128,640]{2,1,0:T(8,128)(2,1)S(1)} %bitcast.140), custom_call_target="tpu_custom_call" | custom-call | tf_op jit(solution)/shard_map/pallas_call | solution.py:493
  108.1 1.2 fusion.40
  109.3 1.8 fusion.36
  111.1 7.7 %shard_map.276 = bf16[4,128,640]{2,1,0:T(8,128)(2,1)S(1)} custom-call(bf16[128,640]{1,0:T(8,128)(2,1)S(1)} %get-tuple-element.112.refs_0_), custom_call_target="tpu_custom_call" | custom-call | tf_op jit(solution)/shard_map/pallas_call | solution.py:493
  118.8 2.5 %multiply_convert_fusion.1 = (bf16[512,512]{1,0:T(8,128)(2,1)S(1)}, bf16[512,512]{1,0:T(8,128)(2,1)S(1)}) fusion(f32[512,512]{1,0:T(8,128)S(1)} %copy-done.19, f32[512,512]{1,0:T(8,128)} %get-tuple-element.137, bf16[512,640]{1,0:T(8,128)(2,1)S(1)} %bitcast.135, bf16[512,640]{1,0:T(8,128)(2,1)S(1)} %bitcast.149), kind=kOutput, calls=%fused_computation.35 | convolution fusion | flops 341835776 | bytes 4456448 | tf_op jit(solution)/shard_map/dot_general | solution.py:668
  124.0 15.0 %shard_map.277 = (f32[128,640]{1,0:T(8,128)S(1)}, bf16[64,640]{1,0:T(8,128)(2,1)S(1)}) custom-call(bf16[4,128,640]{2,1,0:T(8,128)(2,1)S(1)} %bitcast.128, bf16[8,64,640]{2,1,0:T(8,128)(2,1)S(1)} %bitcast.137), custom_call_target="tpu_custom_call" | custom-call | tf_op jit(solution)/shard_map/pallas_call | solution.py:493
  140.1 13.9 %shard_map.278 = (bf16[4,128,640]{2,1,0:T(8,128)(2,1)S(1)}, bf16[80,512]{1,0:T(8,128)(2,1)S(1)}) custom-call(bf16[128,640]{1,0:T(8,128)(2,1)S(1)} %fusion.37.refs_0_, bf16[8,80,512]{2,1,0:T(8,128)(2,1)S(1)} %bitcast.138), custom_call_target="tpu_custom_call" | custom-call | tf_op jit(solution)/shard_map/pallas_call | solution.py:493
  154.8 1.1 copy-done.8
  157.8 1.9 multiply_cosine_fusion
  160.2 1.5 convolution_convert_fusion
  162.4 13.7 %shard_map.279 = (f32[128,1152]{1,0:T(8,128)S(1)}, bf16[80,512]{1,0:T(8,128)(2,1)S(1)}) custom-call(bf16[4,128,1152]{2,1,0:T(8,128)(2,1)S(1)} %pad_maximum_fusion.refs_0_, bf16[8,80,512]{2,1,0:T(8,128)(2,1)S(1)} %bitcast.134), custom_call_target="tpu_custom_call" | custom-call | tf_op jit(solution)/shard_map/pallas_call | solution.py:493
  178.0 1.1 multiply_reduce_fusion.12
  180.1 1.6 fusion.34
  183.8 11.4 %shard_map.280 = (bf16[4,128,512]{2,1,0:T(8,128)(2,1)S(1)}, bf16[4,64,640]{2,1,0:T(8,128)(2,1)S(1)}, bf16[80,256]{1,0:T(8,128)(2,1)S(1)}) custom-call(bf16[128,512]{1,0:T(8,128)(2,1)S(1)} %pad_maximum_fusion.7.refs_0_, bf16[4,64,640]{2,1,0:T(8,128)(2,1)S(1)} %bitcast.129, bf16[8,80,256]{2,1,0:T(8,128)(2,1)S(1)} %bitcast.146), custom_call_target="tpu_custom_call" | custom-call | tf_op jit(solution)/shard_map/pallas_call | solution.py:493
  196.3 16.8 %shard_map.281 = (bf16[4,32,640]{2,1,0:T(8,128)(2,1)S(1)}, bf16[4,80,128]{2,1,0:T(8,128)(2,1)S(1)}, bf16[4,16,384]{2,1,0:T(8,128)(2,1)S(1)}, bf16[4,80,512]{2,1,...) custom-call(bf16[8,32,640]{2,1,0:T(8,128)(2,1)S(1)} %bitcast.144, ...), custom_call_target="tpu_custom_call" | custom-call | tf_op jit(solution)/shard_map/pallas_call | solution.py:616
  217.5 1.5 copy.46
  219.0 2.4 %copy.48 = f32[80,2048]{1,0:T(8,128)} copy(f32[80,2048]{0,1:T(8,128)} %bitcast.155) | data formatting | bytes 1310720
  222.1 1.2 copy.49
  (164 shorter events, 30.1 us)
Async XLA Ops:
  0.6 83.8 %copy-start = (bf16[256,640]{1,0:T(8,128)(2,1)S(1)}, bf16[256,640]{1,0:T(8,128)(2,1)}, u32[]{:S(2)}) copy-start(bf16[256,640]{1,0:T(8,128)(2,1)} %param.30) | copy-start | bytes 983044
  0.7 37.6 %copy-start.23 = (bf16[80,2048]{1,0:T(8,128)(2,1)S(1)}, bf16[80,2048]{1,0:T(8,128)(2,1)}, u32[]{:S(2)}) copy-start(bf16[80,2048]{1,0:T(8,128)(2,1)} %param.29) | copy-start | bytes 983044
  35.3 5.2 %copy-start.4 = (bf16[8,32,640]{2,1,0:T(8,128)(2,1)}, bf16[8,32,640]{2,1,0:T(8,128)(2,1)S(1)}, u32[]{:S(2)}) copy-start(bf16[8,32,640]{2,1,0:T(8,128)(2,1)S(1)} %get-tuple-element.42) | copy-start | bytes 983044
  40.6 1.0 copy-start.5
  58.1 1.9 copy-start.9
  65.3 0.7 copy-start.28
  65.3 0.8 copy-start.30
  66.1 1.8 copy-start.10
  67.9 0.8 copy-start.16
  67.9 1.0 copy-start.22
  68.0 0.7 copy-start.12
  68.0 16.0 %copy-start.14 = (bf16[1,128,640]{2,1,0:T(8,128)(2,1)S(1)}, bf16[1,128,640]{2,1,0:T(8,128)(2,1)}, u32[]{:S(2)}) copy-start(bf16[1,128,640]{2,1,0:T(8,128)(2,1)} %param.16) | copy-start | bytes 491524
  83.0 0.8 copy-start.1
  84.4 14.6 %copy-start.2 = (bf16[8,80,512]{2,1,0:T(8,128)(2,1)S(1)}, bf16[8,80,512]{2,1,0:T(8,128)(2,1)}, u32[]{:S(2)}) copy-start(bf16[8,80,512]{2,1,0:T(8,128)(2,1)} %copy-done.1) | copy-start | bytes 1966084
  98.5 2.3 %copy-start.6 = (bf16[8,64,640]{2,1,0:T(8,128)(2,1)}, bf16[8,64,640]{2,1,0:T(8,128)(2,1)S(1)}, u32[]{:S(2)}) copy-start(bf16[8,64,640]{2,1,0:T(8,128)(2,1)S(1)} %get-tuple-element.50) | copy-start | bytes 1966084
  99.1 1.7 copy-start.18
  100.7 7.2 %copy-start.32 = (bf16[512,512]{1,0:T(8,128)(2,1)}, bf16[512,512]{1,0:T(8,128)(2,1)S(1)}, u32[]{:S(2)}) copy-start(bf16[512,512]{1,0:T(8,128)(2,1)S(1)} %get-tuple-element.136) | copy-start | bytes 1572868
  108.1 10.7 %copy-start.7 = (bf16[8,64,640]{2,1,0:T(8,128)(2,1)S(1)}, bf16[8,64,640]{2,1,0:T(8,128)(2,1)}, u32[]{:S(2)}) copy-start(bf16[8,64,640]{2,1,0:T(8,128)(2,1)} %copy-done.6) | copy-start | bytes 1966084
  108.1 10.7 %copy-start.19 = (f32[512,512]{1,0:T(8,128)S(1)}, f32[512,512]{1,0:T(8,128)}, u32[]{:S(2)}) copy-start(f32[512,512]{1,0:T(8,128)} %copy-done.18) | copy-start | bytes 3145732
  121.3 1.1 copy-start.3
  122.3 1.0 copy-start.33
  124.0 15.2 %copy-start.15 = (bf16[1,128,640]{2,1,0:T(8,128)(2,1)S(1)}, bf16[1,128,640]{2,1,0:T(8,128)(2,1)}, u32[]{:S(2)}) copy-start(bf16[1,128,640]{2,1,0:T(8,128)(2,1)} %param.18) | copy-start | bytes 491524
  139.6 14.4 %copy-start.13 = (bf16[4,2,32,640]{3,2,0,1:T(8,128)(2,1)S(1)}, bf16[4,2,32,640]{3,2,0,1:T(8,128)(2,1)}, u32[]{:S(2)}) copy-start(bf16[4,2,32,640]{3,2,0,1:T(8,128)(2,1)} %copy-done.12) | copy-start | bytes 983044
  140.1 14.3 %copy-start.11 = (f32[512,512]{0,1:T(8,128)S(1)}, f32[512,512]{0,1:T(8,128)}, u32[]{:S(2)}) copy-start(f32[512,512]{0,1:T(8,128)} %copy-done.10) | copy-start | bytes 3145732
  154.4 1.4 copy-start.8
  156.2 0.9 copy-start.29
  156.2 1.0 copy-start.31
  156.2 1.3 copy-start.25
  156.2 1.3 copy-start.27
  160.2 1.5 copy-start.20
  180.1 2.4 %copy-start.17 = (bf16[512,256]{1,0:T(8,128)(2,1)S(1)}, bf16[512,256]{1,0:T(8,128)(2,1)}, u32[]{:S(2)}) copy-start(bf16[512,256]{1,0:T(8,128)(2,1)} %copy-done.16) | copy-start | bytes 786436
  182.5 0.9 copy-start.21
  (2 other events, 1.3 us)

commit v4 on v3

--- a/solution.py
+++ b/solution.py
@@ -355,31 +355,47 @@
         )
 
 
+def row_cuts(axis, rows):
+    cuts = min(3, rows // 16) if axis == "fsdp" else 1
+    edges = [rows // 16 * cut // cuts * 16 for cut in range(cuts)] + [rows]
+    return [(low, high - low) for low, high in zip(edges, edges[1:])]
+
+
 class Gather(Piece):
-    def out(self, source, slot, lane, target):
-        return self.copy(source, self.result.at[slot], lane, target)
+    def rounds(self):
+        return len(row_cuts(self.axis, self.source.shape[0]))
+
+    def out(self, cut, handed, slot, lane, target):
+        low, size = row_cuts(self.axis, self.source.shape[0])[cut]
+        here = pl.ds(low, size)
+        there = self.result.at[slot, here]
+        source = there if handed else self.source.at[here]
+        return self.copy(source, there, cut * (2 * self.span - 1) + lane, target)
 
     def begin(self):
-        for step in range(1, self.span):
-            self.out(self.source, self.me, step, self.ahead(step) * 2 + self.inner).start()
-        self.out(self.source, self.me, 0, self.twin).start()
+        for cut in range(self.rounds()):
+            for step in range(1, self.span):
+                target = self.ahead(step) * 2 + self.inner
+                self.out(cut, False, self.me, step, target).start()
+            self.out(cut, False, self.me, 0, self.twin).start()
 
     def own(self):
         self.result[self.me] = self.source[...]
 
-    def middle(self):
+    def middle(self, cut):
         for step in range(1, self.span):
             slot = self.behind(step) * 2 + self.inner
-            self.out(self.source, slot, step, self.twin).wait_recv()
-            self.out(self.result.at[slot], slot, self.span - 1 + step, self.twin).start()
+            self.out(cut, False, slot, step, self.twin).wait_recv()
+            self.out(cut, True, slot, self.span - 1 + step, self.twin).start()
 
     def end(self):
-        self.out(self.source, self.twin, 0, self.twin).wait_recv()
-        for step in range(1, self.span):
-            slot = self.behind(step) * 2 + (1 - self.inner)
-            self.out(self.source, slot, self.span - 1 + step, self.twin).wait_recv()
-        for lane in range(2 * self.span - 1):
-            self.out(self.source, self.me, lane, self.twin).wait_send()
+        for cut in range(self.rounds()):
+            self.out(cut, False, self.twin, 0, self.twin).wait_recv()
+            for step in range(1, self.span):
+                slot = self.behind(step) * 2 + (1 - self.inner)
+                self.out(cut, False, slot, self.span - 1 + step, self.twin).wait_recv()
+            for lane in range(2 * self.span - 1):
+                self.out(cut, False, self.me, lane, self.twin).wait_send()
 
 
 class Swap(Piece):
@@ -394,7 +410,10 @@
     def own(self):
         self.result[self.me] = self.source[self.me]
 
-    def middle(self):
+    def rounds(self):
+        return 1
+
+    def middle(self, cut):
         pass
 
     def end(self):
@@ -424,7 +443,10 @@
     def own(self):
         pass
 
-    def middle(self):
+    def rounds(self):
+        return 1
+
+    def middle(self, cut):
         from_twin, paired = self.slots[:2]
         for step in range(1, self.span):
             self.to_twin(step).wait_recv()
@@ -470,8 +492,10 @@
         piece.begin()
     for piece in pieces:
         piece.own()
-    for piece in pieces:
-        piece.middle()
+    for cut in range(max(piece.rounds() for piece in pieces)):
+        for piece in pieces:
+            if cut < piece.rounds():
+                piece.middle(cut)
     for piece in pieces:
         piece.end()
 
@@ -489,7 +513,7 @@
         else:
             shapes.append(jax.ShapeDtypeStruct(array.shape[1:], kept))
             slots += [pltpu.VMEM((n // 2,) + array.shape[1:], array.dtype)] * 3
-    lanes = max(n for _, _, n in plan)
+    lanes = 3 * max(n for _, _, n in plan)
     return pl.pallas_call(
         functools.partial(exchange_kernel, plan),
         out_shape=shapes,

time: 225 us -> 231 us (1.027)
  Pallas kernels: 157 us -> 163 us
    pallas_call x10, Pallas kernels: 141 us -> 146 us  [exchange(): pl.pallas_call(functools.partial(exchange_kernel, plan), out_shape=shapes...]
where the time goes in v4:
time: 231 us; the launch traced here: 230 us
  Pallas kernels  163 us (71%)
  local copies, waits for them, and re-layouts  25.4 us (11%)
  other arithmetic  21.5 us (9%)
  matrix products  18.3 us (8%)
    pallas_call x10, Pallas kernels, exchange(): pl.pallas_call(functools.partial(exchange_kernel, plan), out_shape=shapes...  146 us
    dot_general x23, matrix products, mul(): lax.dot_general(left, right, (dims, ((), ())), preferred_element_type=f32)  18.3 us
    pallas_call x1, Pallas kernels, finish(): pl.pallas_call(functools.partial(finish_kernel, owners, ways, sums, count...  17.4 us
    unnamed x73, local copies, waits for them, and re-layouts  11 us

profile of v4, /device:TPU:0, one launch (start us, length us, event | category | flops | bytes accessed | tf_op | source)
XLA Modules:
  0.0 230.1 jit_solution(3264608344790438671)
XLA Ops:
  0.7 4.2 %concatenate.37 = bf16[384]{0:T(512)(128)(2,1)S(1)} concatenate(bf16[80]{0:T(256)(128)(2,1)} %param.19, bf16[80]{0:T(256)(128)(2,1)} %param.26, bf16[80]{0:T(256)(128)(2,1)} %param.27, bf16[80]{0:T(256)(128)(2,1)} %param.31, bf16[32]{0:T(256)(128)(2,1)} %param.23, bf16[32]{0:T(256)(128)(2,1)} %param.24), dimensions={0} | concatenate | bytes 1536 | tf_op jit(solution)/shard_map/concatenate | solution.py:716
  7.2 32.6 %shard_map.271 = (bf16[8,96,768]{2,1,0:T(8,128)(2,1)S(1)}, bf16[8,32,640]{2,1,0:T(8,128)(2,1)S(1)}) custom-call(bf16[96,768]{1,0:T(8,128)(2,1)S(1)} %fusion.59.refs_0_, bf16[32,640]{1,0:T(8,128)(2,1)S(1)} %constant_dynamic-slice_fusion.3.refs_1_), custom_call_target="tpu_custom_call" | custom-call | tf_op jit(solution)/shard_map/pallas_call | solution.py:517
  40.1 1.0 fusion.41
  41.1 1.0 fusion.33.refs_0_
  43.1 1.2 copy.36
  46.1 15.3 %shard_map.272 = (bf16[4,128,640]{2,1,0:T(8,128)(2,1)S(1)}, s32[4,8,128]{2,1,0:T(8,128)S(1)}, bf16[4,64,640]{2,1,0:T(8,128)(2,1)S(1)}, bf16[8,80,512]{2,1,0:T(8,128)(2,1)S(1)}) custom-call(bf16[128,640]{1,0:T(8,128)(2,1)S(1)} %fusion.33.refs_0_, s32[8,128]{1,0:T(8,128)S(1)} %broadcast_in_dim.27.refs_1_, bf16[4,64,640]{2,1,0:T(8,128)(2,1)S(1)} %bitcast.145, ...), custom_call_target="tpu_custom_call" | custom-call | tf_op jit(solution)/shard_map/pallas_call | solution.py:517
  61.6 1.9 fusion.81
  63.6 1.4 multiply_reduce_fusion.4
  65.2 2.1 fusion.75
  67.3 1.4 fusion.46
  69.8 1.6 convolution_convert_fusion.9
  72.6 13.5 %shard_map.273 = (f32[128,640]{1,0:T(8,128)S(1)}, bf16[8,80,512]{2,1,0:T(8,128)(2,1)S(1)}) custom-call(bf16[4,128,640]{2,1,0:T(8,128)(2,1)S(1)} %bitcast.124, bf16[80,512]{1,0:T(8,128)(2,1)S(1)} %copy.51.refs_1_), custom_call_target="tpu_custom_call" | custom-call | tf_op jit(solution)/shard_map/pallas_call | solution.py:517
  87.5 13.2 %shard_map.274 = (bf16[4,128,640]{2,1,0:T(8,128)(2,1)S(1)}, bf16[8,64,640]{2,1,0:T(8,128)(2,1)S(1)}) custom-call(bf16[128,640]{1,0:T(8,128)(2,1)S(1)} %multiply_convert_fusion.3.refs_0_, bf16[64,640]{1,0:T(8,128)(2,1)S(1)} %constant_dynamic-slice_fusion.refs_1_), custom_call_target="tpu_custom_call" | custom-call | tf_op jit(solution)/shard_map/pallas_call | solution.py:517
  101.3 1.6 multiply_convert_fusion.2
  103.5 6.7 %shard_map.275 = f32[128,640]{1,0:T(8,128)S(1)} custom-call(bf16[4,128,640]{2,1,0:T(8,128)(2,1)S(1)} %bitcast.140), custom_call_target="tpu_custom_call" | custom-call | tf_op jit(solution)/shard_map/pallas_call | solution.py:517
  110.5 1.2 fusion.40
  111.7 1.8 fusion.36
  113.4 7.8 %shard_map.276 = bf16[4,128,640]{2,1,0:T(8,128)(2,1)S(1)} custom-call(bf16[128,640]{1,0:T(8,128)(2,1)S(1)} %get-tuple-element.112.refs_0_), custom_call_target="tpu_custom_call" | custom-call | tf_op jit(solution)/shard_map/pallas_call | solution.py:517
  121.3 2.5 %multiply_convert_fusion.1 = (bf16[512,512]{1,0:T(8,128)(2,1)S(1)}, bf16[512,512]{1,0:T(8,128)(2,1)S(1)}) fusion(f32[512,512]{1,0:T(8,128)S(1)} %copy-done.19, f32[512,512]{1,0:T(8,128)} %get-tuple-element.137, bf16[512,640]{1,0:T(8,128)(2,1)S(1)} %bitcast.135, bf16[512,640]{1,0:T(8,128)(2,1)S(1)} %bitcast.149), kind=kOutput, calls=%fused_computation.35 | convolution fusion | flops 341835776 | bytes 4456448 | tf_op jit(solution)/shard_map/dot_general | solution.py:692
  126.5 16.1 %shard_map.277 = (f32[128,640]{1,0:T(8,128)S(1)}, bf16[64,640]{1,0:T(8,128)(2,1)S(1)}) custom-call(bf16[4,128,640]{2,1,0:T(8,128)(2,1)S(1)} %bitcast.128, bf16[8,64,640]{2,1,0:T(8,128)(2,1)S(1)} %bitcast.137), custom_call_target="tpu_custom_call" | custom-call | tf_op jit(solution)/shard_map/pallas_call | solution.py:517
  143.8 13.5 %shard_map.278 = (bf16[4,128,640]{2,1,0:T(8,128)(2,1)S(1)}, bf16[80,512]{1,0:T(8,128)(2,1)S(1)}) custom-call(bf16[128,640]{1,0:T(8,128)(2,1)S(1)} %fusion.37.refs_0_, bf16[8,80,512]{2,1,0:T(8,128)(2,1)S(1)} %bitcast.138), custom_call_target="tpu_custom_call" | custom-call | tf_op jit(solution)/shard_map/pallas_call | solution.py:517
  158.1 1.1 copy-done.8
  161.2 1.9 multiply_cosine_fusion
  163.6 1.5 convolution_convert_fusion
  165.7 14.3 %shard_map.279 = (f32[128,1152]{1,0:T(8,128)S(1)}, bf16[80,512]{1,0:T(8,128)(2,1)S(1)}) custom-call(bf16[4,128,1152]{2,1,0:T(8,128)(2,1)S(1)} %pad_maximum_fusion.refs_0_, bf16[8,80,512]{2,1,0:T(8,128)(2,1)S(1)} %bitcast.134), custom_call_target="tpu_custom_call" | custom-call | tf_op jit(solution)/shard_map/pallas_call | solution.py:517
  182.0 1.1 multiply_reduce_fusion.12
  184.1 1.6 fusion.34
  187.8 12.7 %shard_map.280 = (bf16[4,128,512]{2,1,0:T(8,128)(2,1)S(1)}, bf16[4,64,640]{2,1,0:T(8,128)(2,1)S(1)}, bf16[80,256]{1,0:T(8,128)(2,1)S(1)}) custom-call(bf16[128,512]{1,0:T(8,128)(2,1)S(1)} %pad_maximum_fusion.7.refs_0_, bf16[4,64,640]{2,1,0:T(8,128)(2,1)S(1)} %bitcast.129, bf16[8,80,256]{2,1,0:T(8,128)(2,1)S(1)} %bitcast.146), custom_call_target="tpu_custom_call" | custom-call | tf_op jit(solution)/shard_map/pallas_call | solution.py:517
  201.7 17.4 %shard_map.281 = (bf16[4,32,640]{2,1,0:T(8,128)(2,1)S(1)}, bf16[4,80,128]{2,1,0:T(8,128)(2,1)S(1)}, bf16[4,16,384]{2,1,0:T(8,128)(2,1)S(1)}, bf16[4,80,512]{2,1,...) custom-call(bf16[8,32,640]{2,1,0:T(8,128)(2,1)S(1)} %bitcast.144, ...), custom_call_target="tpu_custom_call" | custom-call | tf_op jit(solution)/shard_map/pallas_call | solution.py:640
  223.4 1.5 copy.46
  224.9 2.4 %copy.48 = f32[80,2048]{1,0:T(8,128)} copy(f32[80,2048]{0,1:T(8,128)} %bitcast.155) | data formatting | bytes 1310720
  228.0 1.2 copy.49
  (164 shorter events, 30.1 us)
Async XLA Ops:
  0.6 86.8 %copy-start = (bf16[256,640]{1,0:T(8,128)(2,1)S(1)}, bf16[256,640]{1,0:T(8,128)(2,1)}, u32[]{:S(2)}) copy-start(bf16[256,640]{1,0:T(8,128)(2,1)} %param.30) | copy-start | bytes 983044
  0.7 42.2 %copy-start.23 = (bf16[80,2048]{1,0:T(8,128)(2,1)S(1)}, bf16[80,2048]{1,0:T(8,128)(2,1)}, u32[]{:S(2)}) copy-start(bf16[80,2048]{1,0:T(8,128)(2,1)} %param.29) | copy-start | bytes 983044
  39.8 5.2 %copy-start.4 = (bf16[8,32,640]{2,1,0:T(8,128)(2,1)}, bf16[8,32,640]{2,1,0:T(8,128)(2,1)S(1)}, u32[]{:S(2)}) copy-start(bf16[8,32,640]{2,1,0:T(8,128)(2,1)S(1)} %get-tuple-element.42) | copy-start | bytes 983044
  45.2 1.0 copy-start.5
  61.5 1.9 copy-start.9
  68.8 0.7 copy-start.28
  68.8 0.8 copy-start.30
  69.6 1.8 copy-start.10
  71.4 0.8 copy-start.16
  71.4 1.0 copy-start.22
  71.5 0.7 copy-start.12
  71.5 15.5 %copy-start.14 = (bf16[1,128,640]{2,1,0:T(8,128)(2,1)S(1)}, bf16[1,128,640]{2,1,0:T(8,128)(2,1)}, u32[]{:S(2)}) copy-start(bf16[1,128,640]{2,1,0:T(8,128)(2,1)} %param.16) | copy-start | bytes 491524
  86.0 0.8 copy-start.1
  87.5 13.8 %copy-start.2 = (bf16[8,80,512]{2,1,0:T(8,128)(2,1)S(1)}, bf16[8,80,512]{2,1,0:T(8,128)(2,1)}, u32[]{:S(2)}) copy-start(bf16[8,80,512]{2,1,0:T(8,128)(2,1)} %copy-done.1) | copy-start | bytes 1966084
  100.7 2.3 copy-start.6
  101.3 1.7 copy-start.18
  103.0 7.3 %copy-start.32 = (bf16[512,512]{1,0:T(8,128)(2,1)}, bf16[512,512]{1,0:T(8,128)(2,1)S(1)}, u32[]{:S(2)}) copy-start(bf16[512,512]{1,0:T(8,128)(2,1)S(1)} %get-tuple-element.136) | copy-start | bytes 1572868
  110.5 10.8 %copy-start.7 = (bf16[8,64,640]{2,1,0:T(8,128)(2,1)S(1)}, bf16[8,64,640]{2,1,0:T(8,128)(2,1)}, u32[]{:S(2)}) copy-start(bf16[8,64,640]{2,1,0:T(8,128)(2,1)} %copy-done.6) | copy-start | bytes 1966084
  110.5 10.8 %copy-start.19 = (f32[512,512]{1,0:T(8,128)S(1)}, f32[512,512]{1,0:T(8,128)}, u32[]{:S(2)}) copy-start(f32[512,512]{1,0:T(8,128)} %copy-done.18) | copy-start | bytes 3145732
  123.8 1.1 copy-start.3
  124.9 1.0 copy-start.33
  126.5 16.3 %copy-start.15 = (bf16[1,128,640]{2,1,0:T(8,128)(2,1)S(1)}, bf16[1,128,640]{2,1,0:T(8,128)(2,1)}, u32[]{:S(2)}) copy-start(bf16[1,128,640]{2,1,0:T(8,128)(2,1)} %param.18) | copy-start | bytes 491524
  143.2 14.1 %copy-start.13 = (bf16[4,2,32,640]{3,2,0,1:T(8,128)(2,1)S(1)}, bf16[4,2,32,640]{3,2,0,1:T(8,128)(2,1)}, u32[]{:S(2)}) copy-start(bf16[4,2,32,640]{3,2,0,1:T(8,128)(2,1)} %copy-done.12) | copy-start | bytes 983044
  143.8 14.0 %copy-start.11 = (f32[512,512]{0,1:T(8,128)S(1)}, f32[512,512]{0,1:T(8,128)}, u32[]{:S(2)}) copy-start(f32[512,512]{0,1:T(8,128)} %copy-done.10) | copy-start | bytes 3145732
  157.8 1.4 copy-start.8
  159.5 0.9 copy-start.29
  159.5 1.0 copy-start.31
  159.5 1.3 copy-start.25
  159.5 1.3 copy-start.27
  163.5 1.5 copy-start.20
  184.1 2.4 %copy-start.17 = (bf16[512,256]{1,0:T(8,128)(2,1)S(1)}, bf16[512,256]{1,0:T(8,128)(2,1)}, u32[]{:S(2)}) copy-start(bf16[512,256]{1,0:T(8,128)(2,1)} %copy-done.16) | copy-start | bytes 786436
  186.5 0.9 copy-start.21
  (2 other events, 1.3 us)
